TPU v7x, 128 devices: a whole 4x4x4 slice. The times are simulated.
128 devices in a mesh: gx: 16 (over z, x_lo, core), gy: 8 (over y, x_hi).
Axes of the slice: x: 4 (x_hi: 2, x_lo: 2; x = x_hi * 2 + x_lo), y: 4, z: 4, core: 2. Of those that a mesh axis runs over, the one named last changes fastest.
Arguments:
- adjoint_forcing: float32 [16, 3072, 3072], P(None, 'gx', 'gy'), may hold values from -6 to 6
- courant_x: bfloat16 [16, 3072, 3072], P(None, 'gx', 'gy'), may hold values from -0.44921875 to 0.44921875
- courant_y: bfloat16 [16, 3072, 3072], P(None, 'gx', 'gy'), may hold values from -0.44921875 to 0.44921875
- vertical_mix: bfloat16 [16, 3072, 3072], P(None, 'gx', 'gy'), may hold values from 0.019897461 to 0.23925781
- tile_block: int32 [32768], replicated, may hold values from 0 to 147455, as said below
- injection_level: int32 [32768], P(('gx', 'gy')), may hold values from 0 to 15
- plume_profile: float32 [16, 16], replicated, may hold values from 0 to 1
- burn_weight: bfloat16 [32768, 6400], P(('gx', 'gy')), may hold values from 0.19921875 to 1
Outputs:
- adjoint_start: float32 [16, 3072, 3072], P(None, 'gx', 'gy')
- emission_gradient: bfloat16 [32768, 6400], P(('gx', 'gy'))
Inputs may be any that keep to these rules, and one draw needn't show every extreme that they name: `tile_block`: the tiles of one device lie on the columns of exactly 64 different devices, exactly 4 of them on each of those.
All inputs are finite; a program needn't handle non-finite values.
Results may differ from a plain program's by a relative error of at most 0.001.
Values sent between devices are 32-bit elements; how exact they have to be, the bound alone decides.
A program may use at most 192 MiB of HBM per device.

v0:
```python
import functools

import jax
import jax.numpy as jnp
from jax import lax
from jax.experimental import pallas as pl
from jax.experimental.pallas import tpu as pltpu
from jax.sharding import PartitionSpec as P

ITERS = 4
TB = 8
SUB = 100
MESH = pl.DeviceIdType.MESH
MIB = 1024 * 1024


def fori(low, high, body):
    def step(i, carry):
        body(i)
        return carry

    lax.fori_loop(low, high, step, 0)


def stencil_kernel(
    f_hbm, cu_hbm, cv_hbm, k_hbm, out,
    field, cu, cv, mix, work, ysend, yrecv,
    load_sem, save_sem, xs_sem, xr_sem, ys_sem, yr_sem,
):
    levels, rows, cols = field.shape
    tiles = cols // 128
    groups = rows // 16
    inner = (groups - 2) // 2
    gx, gy = lax.axis_index("gx"), lax.axis_index("gy")
    nx, ny = lax.axis_size("gx"), lax.axis_size("gy")
    have_x = (gx > 0, gx < nx - 1)
    have_y = (gy > 0, gy < ny - 1)
    peer_x = ((jnp.maximum(gx - 1, 0), gy), (jnp.minimum(gx + 1, nx - 1), gy))
    peer_y = ((gx, jnp.maximum(gy - 1, 0)), (gx, jnp.minimum(gy + 1, ny - 1)))
    lane = lax.broadcasted_iota(jnp.int32, (16, 128), 1)

    pieces = ((0, 16), (rows - 16, 16), (16, 16 * inner), (16 + 16 * inner, 16 * inner))
    loads = []
    for a, (src, dst) in enumerate(((f_hbm, field), (k_hbm, mix))):
        loads.append([
            pltpu.make_async_copy(
                src.at[:, pl.ds(at, size), :], dst.at[:, pl.ds(at, size), :], load_sem.at[a, p]
            )
            for p, (at, size) in enumerate(pieces)
        ])
    saves = [
        pltpu.make_async_copy(
            field.at[:, pl.ds(at, size), :], out.at[:, pl.ds(at, size), :], save_sem.at[p]
        )
        for p, (at, size) in enumerate(pieces)
    ]
    late = [
        pltpu.make_async_copy(cu_hbm, cu, load_sem.at[2, 0]),
        pltpu.make_async_copy(cv_hbm, cv, load_sem.at[2, 1]),
    ]
    for p in range(4):
        loads[0][p].start()
        loads[1][p].start()
    for copy in late:
        copy.start()

    zero_row = jnp.zeros((1, 128), jnp.float32)

    def clear(l):
        for b in range(2):
            for j in range(tiles):
                work[b, l, j, 7:8, :] = zero_row
                work[b, l, j, rows + 8 : rows + 9, :] = zero_row

    fori(0, levels, clear)
    yrecv[...] = jnp.zeros_like(yrecv)

    barrier = pltpu.get_barrier_semaphore()
    for have, peers in ((have_x, peer_x), (have_y, peer_y)):
        for side in range(2):
            @pl.when(have[side])
            def _():
                pl.semaphore_signal(barrier, inc=1, device_id=peers[side], device_id_type=MESH)
    expected = sum(h.astype(jnp.int32) for h in have_x + have_y)
    pl.semaphore_wait(barrier, expected)

    def x_copy(n, side):
        b = lax.rem(n, 2)
        src, dst = ((8, rows + 8), (rows + 7, 7))[side]
        return pltpu.make_async_remote_copy(
            src_ref=work.at[b, :, :, pl.ds(src, 1), :],
            dst_ref=work.at[b, :, :, pl.ds(dst, 1), :],
            send_sem=xs_sem.at[n, side],
            recv_sem=xr_sem.at[n, side],
            device_id=peer_x[side],
            device_id_type=MESH,
        )

    def y_copy(n, side, chunk):
        return pltpu.make_async_remote_copy(
            src_ref=ysend.at[n, side, chunk],
            dst_ref=yrecv.at[n, side, chunk],
            send_sem=ys_sem.at[n, side, chunk],
            recv_sem=yr_sem.at[n, side, chunk],
            device_id=peer_y[side],
            device_id_type=MESH,
        )

    def send_x(n):
        for side in range(2):
            @pl.when(have_x[side])
            def _():
                x_copy(n, side).start()

    def send_y(n, chunk):
        for side in range(2):
            @pl.when(have_y[side])
            def _():
                y_copy(n, side, chunk).start()

    def await_x(n):
        for side in range(2):
            @pl.when(have_x[side])
            def _():
                x_copy(n, 1 - side).wait_recv()

    def await_y(n, chunk):
        for side in range(2):
            @pl.when(have_y[side])
            def _():
                y_copy(n, 1 - side, chunk).wait_recv()

    def await_x_sent(n):
        for side in range(2):
            @pl.when(have_x[side])
            def _():
                x_copy(n, side).wait_send()

    def mixed(values, i, j):
        at = pl.multiple_of(16 * i, 16)
        result, before = [], None
        for l in range(levels):
            total = values[l]
            if l < levels - 1:
                k = mix[l, pl.ds(at, 16), 128 * j : 128 * j + 128].astype(jnp.float32)
                flux = k * (values[l + 1] - values[l])
                total = total + flux
            if before is not None:
                total = total - before
            before = flux
            result.append(total)
        return result

    def store_mixed(n, values, i, j, m, chunk):
        b = lax.rem(n, 2)
        at = pl.multiple_of(8 + 16 * i, 8)
        result = mixed(values, i, j)
        for l in range(levels):
            work[b, l, j, pl.ds(at, 16), :] = result[l]
        for side, tile, own in ((0, 0, 0), (1, tiles - 1, 127)):
            if j == tile:
                packed = result[0] if own == 0 else pltpu.roll(result[0], 1, 1)
                for l in range(1, levels):
                    moved = pltpu.roll(result[l], (l - own) % 128, 1)
                    packed = jnp.where(lane == l, moved, packed)
                packed = pltpu.roll(packed, 16 * m, 1)
                old = ysend[n, side, chunk]
                ysend[n, side, chunk] = jnp.where(lane // 16 == m, packed, old)

    def moved_by_wind(n, i, j, m, chunk):
        b = lax.rem(n + 1, 2)
        at = pl.multiple_of(16 * i, 16)
        here = 8 + 16 * i
        before = after = None
        if j == 0:
            before = pltpu.roll(yrecv[n - 1, 1, chunk], lax.rem(128 - 16 * m, 128), 1)
        if j == tiles - 1:
            after = pltpu.roll(yrecv[n - 1, 0, chunk], lax.rem(128 - 16 * m, 128), 1)
        values = []
        for l in range(levels):
            c = work[b, l, j, pl.ds(here, 16), :]
            up = work[b, l, j, pl.ds(here + 1, 16), :]
            down = work[b, l, j, pl.ds(here - 1, 16), :]
            if j == 0:
                left = pltpu.roll(before, 127 - l, 1)
            else:
                left = work[b, l, j - 1, pl.ds(here, 16), :]
            if j == tiles - 1:
                right = pltpu.roll(after, (128 - l) % 128, 1) if l else after
            else:
                right = work[b, l, j + 1, pl.ds(here, 16), :]
            left = pltpu.roll(jnp.where(lane == 127, left, c), 1, 1)
            right = pltpu.roll(jnp.where(lane == 0, right, c), 127, 1)
            su = cu[l, pl.ds(at, 16), 128 * j : 128 * j + 128].astype(jnp.float32)
            sv = cv[l, pl.ds(at, 16), 128 * j : 128 * j + 128].astype(jnp.float32)
            total = c + jnp.abs(su) * (jnp.where(su > 0, up, down) - c)
            total = total + jnp.abs(sv) * (jnp.where(sv > 0, right, left) - c)
            values.append(total)
        return values

    def run(n, mode):
        def group(i, m, chunk):
            at = pl.multiple_of(16 * i, 16)
            for j in range(tiles):
                if mode == "first":
                    values = [
                        field[l, pl.ds(at, 16), 128 * j : 128 * j + 128] for l in range(levels)
                    ]
                else:
                    values = moved_by_wind(n, i, j, m, chunk)
                if mode == "last":
                    for l in range(levels):
                        field[l, pl.ds(at, 16), 128 * j : 128 * j + 128] = values[l]
                else:
                    store_mixed(n, values, i, j, m, chunk)

        if mode == "first":
            for p in range(2):
                loads[0][p].wait()
                loads[1][p].wait()
        else:
            await_x(n - 1)
            await_y(n - 1, 0)
            if mode == "middle":
                @pl.when(n >= 2)
                def _():
                    await_x_sent(n - 2)
        fori(0, 2, lambda m: group(m * (groups - 1), m, 0))
        if mode == "last":
            saves[0].start()
            saves[1].start()
        else:
            send_x(n)
            send_y(n, 0)

        def chunk_of(c):
            if mode != "first":
                await_y(n - 1, c + 1)
            fori(0, inner, lambda m: group(1 + c * inner + m, m, c + 1))
            if mode != "last":
                send_y(n, c + 1)

        if mode == "first":
            for c in range(2):
                loads[0][2 + c].wait()
                loads[1][2 + c].wait()
                chunk_of(c)
        elif mode == "last":
            for c in range(2):
                chunk_of(c)
                saves[2 + c].start()
        else:
            fori(0, 2, chunk_of)

    run(0, "first")
    for copy in late:
        copy.wait()
    fori(1, ITERS, lambda n: run(n, "middle"))
    run(ITERS, "last")
    for save in saves:
        save.wait()
    for n in (ITERS - 2, ITERS - 1):
        await_x_sent(n)
    for n in range(ITERS):
        for side in range(2):
            @pl.when(have_y[side])
            def _():
                for chunk in range(3):
                    y_copy(n, side, chunk).wait_send()


def stencil(f, cu, cv, k):
    levels, rows, cols = f.shape
    any_space = pl.BlockSpec(memory_space=pl.ANY)
    tiles = cols // 128
    return pl.pallas_call(
        stencil_kernel,
        out_shape=jax.ShapeDtypeStruct(f.shape, jnp.float32),
        in_specs=[any_space] * 4,
        out_specs=any_space,
        scratch_shapes=[
            pltpu.VMEM(f.shape, jnp.float32),
            pltpu.VMEM(f.shape, jnp.bfloat16),
            pltpu.VMEM(f.shape, jnp.bfloat16),
            pltpu.VMEM(f.shape, jnp.bfloat16),
            pltpu.VMEM((2, levels, tiles, rows + 16, 128), jnp.float32),
            pltpu.VMEM((ITERS, 2, 3, 16, 128), jnp.float32),
            pltpu.VMEM((ITERS, 2, 3, 16, 128), jnp.float32),
            pltpu.SemaphoreType.DMA((3, 4)),
            pltpu.SemaphoreType.DMA((4,)),
            pltpu.SemaphoreType.DMA((ITERS, 2)),
            pltpu.SemaphoreType.DMA((ITERS, 2)),
            pltpu.SemaphoreType.DMA((ITERS, 2, 3)),
            pltpu.SemaphoreType.DMA((ITERS, 2, 3)),
        ],
        compiler_params=pltpu.CompilerParams(
            collective_id=0, has_side_effects=True, vmem_limit_bytes=58 * MIB
        ),
        name="stencil",
    )(f, cu, cv, k)


def gather_kernel(table, profile, field, out):
    levels = field.shape[0]
    ny, nx = out.shape[0], out.shape[1]
    lane = lax.broadcasted_iota(jnp.int32, (8, 128), 1)
    sub = lax.broadcasted_iota(jnp.int32, (8, 128), 0)
    mine = lane // 8 % 8 == sub

    def device(d):
        g, p = d // ny, lax.rem(d, ny)
        for pair in range(2):
            found = []
            for h in range(2):
                q = 4 * (4 * d + 2 * pair + h)
                row = pl.multiple_of(table[q], 8)
                col = pl.multiple_of(table[q + 1], 128)
                shift = table[q + 2]
                weight = table[q + 3]
                acc = None
                for l in range(levels):
                    term = profile[weight + l] * field[l, pl.ds(row, 8), pl.ds(col, 128)]
                    acc = term if acc is None else acc + term
                found.append(pltpu.roll(acc, shift, 1))
            both = jnp.where(lane < 64, found[0], found[1])
            for bit in (1, 2, 4):
                both = jnp.where(sub // bit % 2 == 1, pltpu.roll(both, 8 * bit, 1), both)
            both = jnp.where(mine, both, 0.0)
            out[p, g, pair : pair + 1, :] = jnp.sum(both, axis=0, keepdims=True)

    fori(0, nx * ny, device)


def gather(table, profile, field, nx, ny):
    smem = pl.BlockSpec(memory_space=pltpu.SMEM)
    vmem = pl.BlockSpec(memory_space=pltpu.VMEM)
    return pl.pallas_call(
        gather_kernel,
        out_shape=jax.ShapeDtypeStruct((ny, nx, 2, 128), jnp.float32),
        in_specs=[smem, smem, vmem],
        out_specs=vmem,
        compiler_params=pltpu.CompilerParams(vmem_limit_bytes=24 * MIB),
        name="gather",
    )(table, profile, field)


def exchange_kernel(rows, out, held, send1, recv1, send2, recv2):
    ny, nx = rows.shape[0], rows.shape[1]
    gx, gy = lax.axis_index("gx"), lax.axis_index("gy")
    barrier = pltpu.get_barrier_semaphore()

    def greet_y(o):
        pl.semaphore_signal(
            barrier, inc=1, device_id=(gx, lax.rem(gy + o, ny)), device_id_type=MESH
        )

    def greet_x(o):
        pl.semaphore_signal(
            barrier, inc=1, device_id=(lax.rem(gx + o, nx), gy), device_id_type=MESH
        )

    fori(1, ny, greet_y)
    fori(1, nx, greet_x)
    pl.semaphore_wait(barrier, nx + ny - 2)

    def first(o):
        to = lax.rem(gy + o, ny)
        return pltpu.make_async_remote_copy(
            src_ref=rows.at[to],
            dst_ref=held.at[gy],
            send_sem=send1.at[o],
            recv_sem=recv1.at[o],
            device_id=(gx, to),
            device_id_type=MESH,
        )

    def second(o):
        to = lax.rem(gx + o, nx)
        return pltpu.make_async_remote_copy(
            src_ref=held.at[:, to],
            dst_ref=out.at[gx],
            send_sem=send2.at[o],
            recv_sem=recv2.at[o],
            device_id=(to, gy),
            device_id_type=MESH,
        )

    fori(1, ny, lambda o: first(o).start())
    held[gy] = rows[gy]
    fori(1, ny, lambda o: first(o).wait_recv())
    fori(1, nx, lambda o: second(o).start())
    out[gx] = held[:, gx]
    fori(1, nx, lambda o: second(o).wait_recv())
    fori(1, ny, lambda o: first(o).wait_send())
    fori(1, nx, lambda o: second(o).wait_send())


def exchange(rows):
    ny, nx = rows.shape[0], rows.shape[1]
    vmem = pl.BlockSpec(memory_space=pltpu.VMEM)
    return pl.pallas_call(
        exchange_kernel,
        out_shape=jax.ShapeDtypeStruct((nx, ny, 2, 128), jnp.float32),
        in_specs=[vmem],
        out_specs=vmem,
        scratch_shapes=[
            pltpu.VMEM(rows.shape, jnp.float32),
            pltpu.SemaphoreType.DMA((ny,)),
            pltpu.SemaphoreType.DMA((ny,)),
            pltpu.SemaphoreType.DMA((nx,)),
            pltpu.SemaphoreType.DMA((nx,)),
        ],
        compiler_params=pltpu.CompilerParams(
            collective_id=1, has_side_effects=True, vmem_limit_bytes=16 * MIB
        ),
        name="exchange",
    )(rows)


def gradient_kernel(rows, where, burn, out, column):
    step = pl.program_id(0)
    tiles_dev, width = burn.shape

    @pl.when(step == 0)
    def _():
        values = rows[...]
        high = values.astype(jnp.bfloat16)
        rest = values - high.astype(jnp.float32)
        mid = rest.astype(jnp.bfloat16)
        low = (rest - mid.astype(jnp.float32)).astype(jnp.bfloat16)
        index = where[:, 0:1]
        half = where[:, 1:2]
        count = values.shape[0]
        onehot = (lax.broadcasted_iota(jnp.int32, (tiles_dev, count), 1) == index).astype(
            jnp.float32
        ).astype(jnp.bfloat16)
        lane = lax.broadcasted_iota(jnp.int32, (tiles_dev, 128), 1)
        parts = []
        for part in (high, mid, low):
            picked = jnp.dot(onehot, part, preferred_element_type=jnp.float32)
            parts.append(jnp.where(half == 1, pltpu.roll(picked, 64, 1), picked))
        column[:, 0:128] = jnp.where(lane < 64, parts[0], pltpu.roll(parts[1], 64, 1)).astype(
            jnp.bfloat16
        )
        column[:, 128:256] = jnp.where(lane < 64, parts[2], 0.0).astype(jnp.bfloat16)

    cell = step * width + lax.broadcasted_iota(jnp.int32, (64, width), 1)
    start = SUB * lax.broadcasted_iota(jnp.int32, (64, width), 0)
    spread = ((cell >= start) & (cell < start + SUB)).astype(jnp.float32).astype(jnp.bfloat16)
    spread = jnp.concatenate([spread] * 4, axis=0)
    expanded = jnp.dot(column[...], spread, preferred_element_type=jnp.float32)
    out[...] = (burn[...].astype(jnp.float32) * expanded).astype(jnp.bfloat16)


def gradient(rows, where, burn):
    tiles_dev, fire = burn.shape
    width = 1280
    return pl.pallas_call(
        gradient_kernel,
        grid=(fire // width,),
        out_shape=jax.ShapeDtypeStruct(burn.shape, jnp.bfloat16),
        in_specs=[
            pl.BlockSpec(rows.shape, lambda s: (0, 0)),
            pl.BlockSpec(where.shape, lambda s: (0, 0)),
            pl.BlockSpec((tiles_dev, width), lambda s: (0, s)),
        ],
        out_specs=pl.BlockSpec((tiles_dev, width), lambda s: (0, s)),
        scratch_shapes=[pltpu.VMEM((tiles_dev, 256), jnp.bfloat16)],
        compiler_params=pltpu.CompilerParams(vmem_limit_bytes=24 * MIB),
        name="gradient",
    )(rows, where, burn)


def locate(block_ids, per_x, per_y, blocks_y, gy_count):
    block_row = block_ids // blocks_y
    block_col = block_ids % blocks_y
    source = block_row // per_x * gy_count + block_col // per_y
    local_block = block_row % per_x * per_y + block_col % per_y
    return (source, local_block)


def on_device(
    adjoint_forcing,
    courant_x,
    courant_y,
    vertical_mix,
    tile_block,
    injection_level,
    plume_profile,
    burn_weight,
):
    levels, width_x, width_y = adjoint_forcing.shape
    gx_count = lax.axis_size("gx")
    gy_count = lax.axis_size("gy")
    total = gx_count * gy_count
    tiles_dev = injection_level.shape[0]
    capacity = 4
    per_x = width_x // TB
    per_y = width_y // TB
    blocks_y = per_y * gy_count
    me = lax.axis_index(("gx", "gy"))
    all_levels = lax.all_gather(injection_level, ("gx", "gy"), tiled=True).reshape(total, tiles_dev)
    slot_table = tile_block.reshape(total, tiles_dev)
    source, local_block = locate(slot_table, per_x, per_y, blocks_y, gy_count)
    is_mine = (source == me).astype(jnp.int32)
    upto = jnp.triu(jnp.ones((tiles_dev, tiles_dev), jnp.bfloat16))
    rank = jnp.dot(
        is_mine.astype(jnp.bfloat16), upto, preferred_element_type=jnp.float32
    ).astype(jnp.int32) - 1
    slots = jnp.arange(capacity, dtype=jnp.int32)
    hits = (is_mine[:, None, :] == 1) & (rank[:, None, :] == slots[None, :, None])
    local = jnp.sum(jnp.where(hits, local_block[:, None, :], 0), axis=2)
    level = jnp.sum(jnp.where(hits, all_levels[:, None, :], 0), axis=2)
    block_row = local // per_y
    lane_at = local % per_y * TB
    shift = (64 * (slots % 2)[None, :] - lane_at) % 128
    table = jnp.stack(
        [block_row * TB, lane_at // 128 * 128, shift, level * levels], axis=2
    ).reshape(-1)

    state_field = stencil(adjoint_forcing, courant_x, courant_y, vertical_mix)
    rows = gather(table, plume_profile.reshape(-1), state_field, gx_count, gy_count)
    rows = exchange(rows).reshape(total * 2, 128)

    own = lax.dynamic_slice_in_dim(source, me, 1, 0).reshape(tiles_dev)
    positions = jnp.arange(tiles_dev, dtype=jnp.int32)
    earlier = (own[None, :] == own[:, None]) & (positions[None, :] <= positions[:, None])
    arrival = jnp.sum(earlier.astype(jnp.int32), axis=1) - 1
    where = jnp.stack([own * 2 + arrival // 2, arrival % 2], axis=1)
    return (state_field, gradient(rows, where, burn_weight))


def solution(mesh):
    return jax.shard_map(
        on_device,
        mesh=mesh,
        in_specs=(
            P(None, "gx", "gy"),
            P(None, "gx", "gy"),
            P(None, "gx", "gy"),
            P(None, "gx", "gy"),
            P(),
            P(("gx", "gy")),
            P(),
            P(("gx", "gy"), None),
        ),
        out_specs=(P(None, "gx", "gy"), P(("gx", "gy"), None)),
        check_vma=False,
    )
```

profile of v0, /device:TPU:1, one launch (start us, length us, event | category | flops | bytes accessed | tf_op | source)
XLA Modules:
  0.0 431.0 jit_solution(18375829057752237870)
XLA Ops:
  0.6 0.8 reshape.363.profile
  1.4 0.9 sign_compare_fusion.2
  2.4 309.8 %all-gather = s32[128,1,256]{2,1,0:T(1,128)S(1)} all-gather(s32[1,1,256]{2,1,0:T(1,128)} %bitcast.39), channel_id=1, replica_groups=mesh['gx'=16,'gy'=8] {'gx','gy'}, dimensions={0}, use_global_device_ids=true | all-gather | bytes 132096 | tf_op jit(solution)/shard_map/all_gather | solution.py:502
  312.3 1.0 broadcast_divide_fusion
  313.3 0.2 fusion.7
  313.5 0.3 convert_compare_fusion
  313.8 0.2 convert_reduce_fusion
  314.0 0.1 copy.26.where
  314.2 0.2 fusion
  314.4 0.3 select_reduce_fusion.1
  314.8 0.1 fusion.14
  314.8 0.2 copy.25
  315.0 0.3 reshape.362.table
  315.3 50.1 %stencil.1.field = f32[16,192,384]{2,1,0:T(8,128)} custom-call(f32[16,192,384]{2,1,0:T(8,128)} %f_hbm.1, bf16[16,192,384]{2,1,0:T(8,128)(2,1)} %cu_hbm.1, bf16[16,192,384]{2,1,0:T(8,128)(2,1)} %cv_hbm.1, bf16[16,192,384]{2,1,0:T(8,128)(2,1)} %k_hbm.1), custom_call_target="tpu_custom_call" | custom-call | tf_op jit(solution)/shard_map/stencil/pallas_call | solution.py:276
  365.4 0.0 copy-start
  365.4 2.3 copy-done
  367.7 0.0 copy-start.2
  367.7 43.5 %gather.1.rows = f32[8,16,2,128]{3,2,1,0:T(2,128)S(1)} custom-call(s32[2048]{0:T(1024)S(1)} %reshape.362.table, f32[256]{0:T(256)S(1)} %reshape.363.profile, f32[16,192,384]{2,1,0:T(8,128)S(1)} %copy-done), custom_call_target="tpu_custom_call" | custom-call | tf_op jit(solution)/shard_map/gather/pallas_call | solution.py:337
  411.2 13.4 %exchange.1 = f32[16,8,2,128]{3,2,1,0:T(2,128)S(1)} custom-call(f32[8,16,2,128]{3,2,1,0:T(2,128)S(1)} %gather.1.rows), custom_call_target="tpu_custom_call" | custom-call | tf_op jit(solution)/shard_map/exchange/pallas_call | solution.py:401
  424.6 0.0 copy-done.2
  424.6 0.0 copy-start.1
  424.6 4.2 gradient.1
  428.8 0.0 copy-done.1
  428.8 2.2 copy.34
  (12 shorter events, 0.2 us)
Async XLA Ops:
  365.4 2.3 copy-start
  367.7 56.9 %copy-start.2 = (bf16[256,6400]{1,0:T(8,128)(2,1)S(1)}, bf16[256,6400]{1,0:T(8,128)(2,1)}, u32[]{:S(2)}) copy-start(bf16[256,6400]{1,0:T(8,128)(2,1)} %burn.1) | copy-start | bytes 9830404
  424.6 4.2 copy-start.1
where the time goes:
time: 431 us
  blocking collectives  310 us (72%)
  Pallas kernels  111 us (26%)
  local copies, waits for them, and re-layouts  6 us (1%)
    all_gather x1, blocking collectives, on_device(): lax.all_gather(injection_level, ('gx', 'gy'), tiled=True)  310 us
    pallas_call x1, Pallas kernels, stencil(): pl.pallas_call(stencil_kernel, out_shape=jax.ShapeDtypeStruct(f.shape, jn...  50.1 us
    pallas_call x1, Pallas kernels, gather(): pl.pallas_call(gather_kernel, out_shape=jax.ShapeDtypeStruct((ny, nx, 2,...  43.5 us
    pallas_call x1, Pallas kernels, exchange(): pl.pallas_call(exchange_kernel, out_shape=jax.ShapeDtypeStruct((nx, ny, 2...  13.4 us

commit v1 on v0

--- a/solution.py
+++ b/solution.py
@@ -23,14 +23,16 @@
 
 
 def stencil_kernel(
-    f_hbm, cu_hbm, cv_hbm, k_hbm, out,
-    field, cu, cv, mix, work, ysend, yrecv,
+    f_hbm, cu_hbm, cv_hbm, k_hbm, own, out, shared,
+    field, cu, cv, mix, work, ysend, yrecv, held,
     load_sem, save_sem, xs_sem, xr_sem, ys_sem, yr_sem,
+    send1, recv1, send2, recv2,
 ):
     levels, rows, cols = field.shape
     tiles = cols // 128
     groups = rows // 16
-    inner = (groups - 2) // 2
+    chunks = groups // 2
+    early = max(1, (chunks - 1) // 2)
     gx, gy = lax.axis_index("gx"), lax.axis_index("gy")
     nx, ny = lax.axis_size("gx"), lax.axis_size("gy")
     have_x = (gx > 0, gx < nx - 1)
@@ -38,29 +40,31 @@
     peer_x = ((jnp.maximum(gx - 1, 0), gy), (jnp.minimum(gx + 1, nx - 1), gy))
     peer_y = ((gx, jnp.maximum(gy - 1, 0)), (gx, jnp.minimum(gy + 1, ny - 1)))
     lane = lax.broadcasted_iota(jnp.int32, (16, 128), 1)
-
-    pieces = ((0, 16), (rows - 16, 16), (16, 16 * inner), (16 + 16 * inner, 16 * inner))
-    loads = []
-    for a, (src, dst) in enumerate(((f_hbm, field), (k_hbm, mix))):
-        loads.append([
+    odd = lane % 2 == 1
+
+    pieces = [(0, 16, 0), (rows - 16, 16, 0), (16, 32 * early, 1)]
+    if chunks - 1 > early:
+        pieces.append((16 + 32 * early, 32 * (chunks - 1 - early), 1 + early))
+    bounds = sorted({first for _, _, first in pieces}) + [chunks]
+
+    def parts_copy(src, dst, sem):
+        return [
             pltpu.make_async_copy(
-                src.at[:, pl.ds(at, size), :], dst.at[:, pl.ds(at, size), :], load_sem.at[a, p]
+                src.at[:, pl.ds(at, size), :], dst.at[:, pl.ds(at, size), :], sem.at[p]
             )
-            for p, (at, size) in enumerate(pieces)
-        ])
-    saves = [
-        pltpu.make_async_copy(
-            field.at[:, pl.ds(at, size), :], out.at[:, pl.ds(at, size), :], save_sem.at[p]
-        )
-        for p, (at, size) in enumerate(pieces)
-    ]
+            for p, (at, size, _) in enumerate(pieces)
+        ]
+
+    load_f = parts_copy(f_hbm, field, load_sem.at[0])
+    load_k = parts_copy(k_hbm, mix, load_sem.at[1])
+    saves = parts_copy(field, out, save_sem)
     late = [
         pltpu.make_async_copy(cu_hbm, cu, load_sem.at[2, 0]),
         pltpu.make_async_copy(cv_hbm, cv, load_sem.at[2, 1]),
     ]
-    for p in range(4):
-        loads[0][p].start()
-        loads[1][p].start()
+    for p in range(len(pieces)):
+        load_f[p].start()
+        load_k[p].start()
     for copy in late:
         copy.start()
 
@@ -76,13 +80,43 @@
     yrecv[...] = jnp.zeros_like(yrecv)
 
     barrier = pltpu.get_barrier_semaphore()
-    for have, peers in ((have_x, peer_x), (have_y, peer_y)):
-        for side in range(2):
-            @pl.when(have[side])
-            def _():
-                pl.semaphore_signal(barrier, inc=1, device_id=peers[side], device_id_type=MESH)
-    expected = sum(h.astype(jnp.int32) for h in have_x + have_y)
-    pl.semaphore_wait(barrier, expected)
+
+    def greet_y(o):
+        pl.semaphore_signal(
+            barrier, inc=1, device_id=(gx, lax.rem(gy + o, ny)), device_id_type=MESH
+        )
+
+    def greet_x(o):
+        pl.semaphore_signal(
+            barrier, inc=1, device_id=(lax.rem(gx + o, nx), gy), device_id_type=MESH
+        )
+
+    fori(1, ny, greet_y)
+    fori(1, nx, greet_x)
+    pl.semaphore_wait(barrier, nx + ny - 2)
+
+    def share_y(o):
+        return pltpu.make_async_remote_copy(
+            src_ref=own,
+            dst_ref=held.at[gy],
+            send_sem=send1.at[o],
+            recv_sem=recv1.at[o],
+            device_id=(gx, lax.rem(gy + o, ny)),
+            device_id_type=MESH,
+        )
+
+    def share_x(o):
+        return pltpu.make_async_remote_copy(
+            src_ref=held,
+            dst_ref=shared.at[gx],
+            send_sem=send2.at[o],
+            recv_sem=recv2.at[o],
+            device_id=(lax.rem(gx + o, nx), gy),
+            device_id_type=MESH,
+        )
+
+    fori(1, ny, lambda o: share_y(o).start())
+    held[gy] = own[...]
 
     def x_copy(n, side):
         b = lax.rem(n, 2)
@@ -98,7 +132,7 @@
 
     def y_copy(n, side, chunk):
         return pltpu.make_async_remote_copy(
-            src_ref=ysend.at[n, side, chunk],
+            src_ref=ysend.at[n, chunk],
             dst_ref=yrecv.at[n, side, chunk],
             send_sem=ys_sem.at[n, side, chunk],
             recv_sem=yr_sem.at[n, side, chunk],
@@ -136,8 +170,7 @@
             def _():
                 x_copy(n, side).wait_send()
 
-    def mixed(values, i, j):
-        at = pl.multiple_of(16 * i, 16)
+    def mixed(values, at, j):
         result, before = [], None
         for l in range(levels):
             total = values[l]
@@ -151,44 +184,25 @@
             result.append(total)
         return result
 
-    def store_mixed(n, values, i, j, m, chunk):
-        b = lax.rem(n, 2)
-        at = pl.multiple_of(8 + 16 * i, 8)
-        result = mixed(values, i, j)
+    def pack(first, last, m):
+        packed = None
         for l in range(levels):
-            work[b, l, j, pl.ds(at, 16), :] = result[l]
-        for side, tile, own in ((0, 0, 0), (1, tiles - 1, 127)):
-            if j == tile:
-                packed = result[0] if own == 0 else pltpu.roll(result[0], 1, 1)
-                for l in range(1, levels):
-                    moved = pltpu.roll(result[l], (l - own) % 128, 1)
-                    packed = jnp.where(lane == l, moved, packed)
-                packed = pltpu.roll(packed, 16 * m, 1)
-                old = ysend[n, side, chunk]
-                ysend[n, side, chunk] = jnp.where(lane // 16 == m, packed, old)
-
-    def moved_by_wind(n, i, j, m, chunk):
-        b = lax.rem(n + 1, 2)
-        at = pl.multiple_of(16 * i, 16)
-        here = 8 + 16 * i
-        before = after = None
-        if j == 0:
-            before = pltpu.roll(yrecv[n - 1, 1, chunk], lax.rem(128 - 16 * m, 128), 1)
-        if j == tiles - 1:
-            after = pltpu.roll(yrecv[n - 1, 0, chunk], lax.rem(128 - 16 * m, 128), 1)
+            ends = jnp.where(lane == 0, first[l], last[l])
+            if l:
+                moved = pltpu.roll(ends, 2 * l, 1)
+                packed = jnp.where((lane == 2 * l) | (lane == 2 * l - 1), moved, packed)
+            else:
+                packed = ends
+        return packed if m == 0 else pltpu.roll(packed, 32 * m, 1)
+
+    def moved_by_wind(b, at, here, j, halo):
         values = []
         for l in range(levels):
             c = work[b, l, j, pl.ds(here, 16), :]
             up = work[b, l, j, pl.ds(here + 1, 16), :]
             down = work[b, l, j, pl.ds(here - 1, 16), :]
-            if j == 0:
-                left = pltpu.roll(before, 127 - l, 1)
-            else:
-                left = work[b, l, j - 1, pl.ds(here, 16), :]
-            if j == tiles - 1:
-                right = pltpu.roll(after, (128 - l) % 128, 1) if l else after
-            else:
-                right = work[b, l, j + 1, pl.ds(here, 16), :]
+            left = halo[l] if j == 0 else work[b, l, j - 1, pl.ds(here, 16), :]
+            right = halo[l] if j == tiles - 1 else work[b, l, j + 1, pl.ds(here, 16), :]
             left = pltpu.roll(jnp.where(lane == 127, left, c), 1, 1)
             right = pltpu.roll(jnp.where(lane == 0, right, c), 127, 1)
             su = cu[l, pl.ds(at, 16), 128 * j : 128 * j + 128].astype(jnp.float32)
@@ -199,146 +213,204 @@
         return values
 
     def run(n, mode):
-        def group(i, m, chunk):
-            at = pl.multiple_of(16 * i, 16)
-            for j in range(tiles):
+        source, target = lax.rem(n + 1, 2), lax.rem(n, 2)
+
+        def chunk_of(chunk):
+            if mode != "first":
+                await_y(n - 1, chunk)
+            packed = []
+            for m in range(2):
+                i = jnp.where(chunk == 0, m * (groups - 1), 2 * chunk - 1 + m)
+                at = pl.multiple_of(16 * i, 16)
+                here = pl.multiple_of(8 + 16 * i, 8)
+                if mode != "first":
+                    halo = jnp.where(odd, yrecv[n - 1, 1, chunk], yrecv[n - 1, 0, chunk])
+                    halo = [
+                        pltpu.roll(halo, (-32 * m - 2 * l) % 128, 1) if m or l else halo
+                        for l in range(levels)
+                    ]
+                kept = []
+                for j in range(tiles):
+                    if mode == "first":
+                        values = [
+                            field[l, pl.ds(at, 16), 128 * j : 128 * j + 128]
+                            for l in range(levels)
+                        ]
+                    else:
+                        values = moved_by_wind(source, at, here, j, halo)
+                    if mode == "last":
+                        for l in range(levels):
+                            field[l, pl.ds(at, 16), 128 * j : 128 * j + 128] = values[l]
+                    else:
+                        result = mixed(values, at, j)
+                        for l in range(levels):
+                            work[target, l, j, pl.ds(here, 16), :] = result[l]
+                if mode != "last":
+                    ends = [
+                        [work[target, l, j, pl.ds(here, 16), :] for l in range(levels)]
+                        for j in (0, tiles - 1)
+                    ]
+                    packed.append(pack(ends[0], ends[1], m))
+            if mode != "last":
+                ysend[n, chunk] = jnp.where((lane >= 31) & (lane < 63), packed[1], packed[0])
+                send_y(n, chunk)
+
+        def edges_first(chunk):
+            @pl.when(chunk == 0)
+            def _():
+                if mode != "first":
+                    await_x(n - 1)
+                if mode == "middle":
+                    @pl.when(n >= 2)
+                    def _():
+                        await_x_sent(n - 2)
+
+            chunk_of(chunk)
+            if mode != "last":
+                @pl.when(chunk == 0)
+                def _():
+                    send_x(n)
+
+        if mode == "middle":
+            fori(0, chunks, edges_first)
+        else:
+            for low, high in zip(bounds, bounds[1:]):
+                ready = [p for p, piece in enumerate(pieces) if piece[2] == low]
                 if mode == "first":
-                    values = [
-                        field[l, pl.ds(at, 16), 128 * j : 128 * j + 128] for l in range(levels)
-                    ]
-                else:
-                    values = moved_by_wind(n, i, j, m, chunk)
+                    for p in ready:
+                        load_f[p].wait()
+                        load_k[p].wait()
+                fori(low, high, edges_first)
                 if mode == "last":
-                    for l in range(levels):
-                        field[l, pl.ds(at, 16), 128 * j : 128 * j + 128] = values[l]
-                else:
-                    store_mixed(n, values, i, j, m, chunk)
-
-        if mode == "first":
-            for p in range(2):
-                loads[0][p].wait()
-                loads[1][p].wait()
-        else:
-            await_x(n - 1)
-            await_y(n - 1, 0)
-            if mode == "middle":
-                @pl.when(n >= 2)
-                def _():
-                    await_x_sent(n - 2)
-        fori(0, 2, lambda m: group(m * (groups - 1), m, 0))
-        if mode == "last":
-            saves[0].start()
-            saves[1].start()
-        else:
-            send_x(n)
-            send_y(n, 0)
-
-        def chunk_of(c):
-            if mode != "first":
-                await_y(n - 1, c + 1)
-            fori(0, inner, lambda m: group(1 + c * inner + m, m, c + 1))
-            if mode != "last":
-                send_y(n, c + 1)
-
-        if mode == "first":
-            for c in range(2):
-                loads[0][2 + c].wait()
-                loads[1][2 + c].wait()
-                chunk_of(c)
-        elif mode == "last":
-            for c in range(2):
-                chunk_of(c)
-                saves[2 + c].start()
-        else:
-            fori(0, 2, chunk_of)
+                    for p in ready:
+                        saves[p].start()
 
     run(0, "first")
+    fori(1, ny, lambda o: share_y(o).wait_recv())
+    fori(1, nx, lambda o: share_x(o).start())
+    shared[gx] = held[...]
     for copy in late:
         copy.wait()
     fori(1, ITERS, lambda n: run(n, "middle"))
     run(ITERS, "last")
+    fori(1, nx, lambda o: share_x(o).wait_recv())
+    fori(1, ny, lambda o: share_y(o).wait_send())
+    fori(1, nx, lambda o: share_x(o).wait_send())
     for save in saves:
         save.wait()
     for n in (ITERS - 2, ITERS - 1):
         await_x_sent(n)
-    for n in range(ITERS):
+
+    def all_sent(n):
         for side in range(2):
             @pl.when(have_y[side])
             def _():
-                for chunk in range(3):
-                    y_copy(n, side, chunk).wait_send()
-
-
-def stencil(f, cu, cv, k):
+                fori(0, chunks, lambda chunk: y_copy(n, side, chunk).wait_send())
+
+    fori(0, ITERS, all_sent)
+
+
+def stencil(f, cu, cv, k, own, nx, ny):
     levels, rows, cols = f.shape
     any_space = pl.BlockSpec(memory_space=pl.ANY)
+    vmem = pl.BlockSpec(memory_space=pltpu.VMEM)
     tiles = cols // 128
+    chunks = rows // 32
     return pl.pallas_call(
         stencil_kernel,
-        out_shape=jax.ShapeDtypeStruct(f.shape, jnp.float32),
-        in_specs=[any_space] * 4,
-        out_specs=any_space,
+        out_shape=(
+            jax.ShapeDtypeStruct(f.shape, jnp.float32),
+            jax.ShapeDtypeStruct((nx, ny, *own.shape), jnp.int32),
+        ),
+        in_specs=[any_space] * 4 + [vmem],
+        out_specs=(any_space, vmem),
         scratch_shapes=[
             pltpu.VMEM(f.shape, jnp.float32),
             pltpu.VMEM(f.shape, jnp.bfloat16),
             pltpu.VMEM(f.shape, jnp.bfloat16),
             pltpu.VMEM(f.shape, jnp.bfloat16),
             pltpu.VMEM((2, levels, tiles, rows + 16, 128), jnp.float32),
-            pltpu.VMEM((ITERS, 2, 3, 16, 128), jnp.float32),
-            pltpu.VMEM((ITERS, 2, 3, 16, 128), jnp.float32),
+            pltpu.VMEM((ITERS, chunks, 16, 128), jnp.float32),
+            pltpu.VMEM((ITERS, 2, chunks, 16, 128), jnp.float32),
+            pltpu.VMEM((ny, *own.shape), jnp.int32),
             pltpu.SemaphoreType.DMA((3, 4)),
             pltpu.SemaphoreType.DMA((4,)),
             pltpu.SemaphoreType.DMA((ITERS, 2)),
             pltpu.SemaphoreType.DMA((ITERS, 2)),
-            pltpu.SemaphoreType.DMA((ITERS, 2, 3)),
-            pltpu.SemaphoreType.DMA((ITERS, 2, 3)),
+            pltpu.SemaphoreType.DMA((ITERS, 2, chunks)),
+            pltpu.SemaphoreType.DMA((ITERS, 2, chunks)),
+            pltpu.SemaphoreType.DMA((ny,)),
+            pltpu.SemaphoreType.DMA((ny,)),
+            pltpu.SemaphoreType.DMA((nx,)),
+            pltpu.SemaphoreType.DMA((nx,)),
         ],
         compiler_params=pltpu.CompilerParams(
             collective_id=0, has_side_effects=True, vmem_limit_bytes=58 * MIB
         ),
         name="stencil",
-    )(f, cu, cv, k)
-
-
-def gather_kernel(table, profile, field, out):
+    )(f, cu, cv, k, own)
+
+
+def gather_kernel(table, profile, field, out, weights, sums):
     levels = field.shape[0]
     ny, nx = out.shape[0], out.shape[1]
     lane = lax.broadcasted_iota(jnp.int32, (8, 128), 1)
     sub = lax.broadcasted_iota(jnp.int32, (8, 128), 0)
-    mine = lane // 8 % 8 == sub
-
-    def device(d):
-        g, p = d // ny, lax.rem(d, ny)
-        for pair in range(2):
-            found = []
-            for h in range(2):
-                q = 4 * (4 * d + 2 * pair + h)
-                row = pl.multiple_of(table[q], 8)
-                col = pl.multiple_of(table[q + 1], 128)
-                shift = table[q + 2]
-                weight = table[q + 3]
-                acc = None
-                for l in range(levels):
-                    term = profile[weight + l] * field[l, pl.ds(row, 8), pl.ds(col, 128)]
-                    acc = term if acc is None else acc + term
-                found.append(pltpu.roll(acc, shift, 1))
-            both = jnp.where(lane < 64, found[0], found[1])
-            for bit in (1, 2, 4):
-                both = jnp.where(sub // bit % 2 == 1, pltpu.roll(both, 8 * bit, 1), both)
-            both = jnp.where(mine, both, 0.0)
-            out[p, g, pair : pair + 1, :] = jnp.sum(both, axis=0, keepdims=True)
-
-    fori(0, nx * ny, device)
+
+    def spread(r):
+        for l in range(levels):
+            weights[r, l] = jnp.full((8, 128), profile[r * levels + l], jnp.float32)
+
+    fori(0, profile.shape[0] // levels, spread)
+
+    def weigh(d):
+        for h in range(4):
+            q = 4 * (4 * d + h)
+            row = pl.multiple_of(table[q], 8)
+            col = pl.multiple_of(table[q + 1], 128)
+            r = table[q + 3]
+            terms = [
+                weights[r, l] * field[l, pl.ds(row, 8), pl.ds(col, 128)] for l in range(levels)
+            ]
+            while len(terms) > 1:
+                terms = [a + b for a, b in zip(terms[::2], terms[1::2])]
+            sums[4 * d + h] = terms[0]
+
+    fori(0, nx * ny, weigh)
+
+    def flatten(c):
+        d0 = lax.rem(c, nx // unroll) * unroll, c // (nx // unroll)
+        for u in range(unroll):
+            g, p = d0[0] + u, d0[1]
+            s0 = 4 * (g * ny + p)
+            for pair in range(2):
+                found = []
+                for h in range(2):
+                    s = s0 + 2 * pair + h
+                    found.append(pltpu.roll(sums[s], table[4 * s + 2], 1))
+                both = jnp.where(lane < 64, found[0], found[1])
+                for bit in (1, 2, 4):
+                    both = jnp.where(sub // bit % 2 == 1, pltpu.roll(both, 8 * bit, 1), both)
+                both = jnp.where(lane // 8 % 8 == sub, both, 0.0)
+                out[p, g, pair : pair + 1, :] = jnp.sum(both, axis=0, keepdims=True)
+
+    unroll = 4
+    fori(0, nx * ny // unroll, flatten)
 
 
 def gather(table, profile, field, nx, ny):
     smem = pl.BlockSpec(memory_space=pltpu.SMEM)
     vmem = pl.BlockSpec(memory_space=pltpu.VMEM)
+    levels = field.shape[0]
     return pl.pallas_call(
         gather_kernel,
         out_shape=jax.ShapeDtypeStruct((ny, nx, 2, 128), jnp.float32),
         in_specs=[smem, smem, vmem],
         out_specs=vmem,
+        scratch_shapes=[
+            pltpu.VMEM((profile.shape[0] // levels, levels, 8, 128), jnp.float32),
+            pltpu.VMEM((4 * nx * ny, 8, 128), jnp.float32),
+        ],
         compiler_params=pltpu.CompilerParams(vmem_limit_bytes=24 * MIB),
         name="gather",
     )(table, profile, field)
@@ -499,7 +571,6 @@
     per_y = width_y // TB
     blocks_y = per_y * gy_count
     me = lax.axis_index(("gx", "gy"))
-    all_levels = lax.all_gather(injection_level, ("gx", "gy"), tiled=True).reshape(total, tiles_dev)
     slot_table = tile_block.reshape(total, tiles_dev)
     source, local_block = locate(slot_table, per_x, per_y, blocks_y, gy_count)
     is_mine = (source == me).astype(jnp.int32)
@@ -510,15 +581,19 @@
     slots = jnp.arange(capacity, dtype=jnp.int32)
     hits = (is_mine[:, None, :] == 1) & (rank[:, None, :] == slots[None, :, None])
     local = jnp.sum(jnp.where(hits, local_block[:, None, :], 0), axis=2)
-    level = jnp.sum(jnp.where(hits, all_levels[:, None, :], 0), axis=2)
     block_row = local // per_y
     lane_at = local % per_y * TB
     shift = (64 * (slots % 2)[None, :] - lane_at) % 128
+
+    state_field, all_levels = stencil(
+        adjoint_forcing, courant_x, courant_y, vertical_mix,
+        injection_level.reshape(-1, min(tiles_dev, 128)), gx_count, gy_count,
+    )
+    all_levels = all_levels.reshape(total, tiles_dev)
+    level = jnp.sum(jnp.where(hits, all_levels[:, None, :], 0), axis=2)
     table = jnp.stack(
-        [block_row * TB, lane_at // 128 * 128, shift, level * levels], axis=2
+        [block_row * TB, lane_at // 128 * 128, shift, level], axis=2
     ).reshape(-1)
-
-    state_field = stencil(adjoint_forcing, courant_x, courant_y, vertical_mix)
     rows = gather(table, plume_profile.reshape(-1), state_field, gx_count, gy_count)
     rows = exchange(rows).reshape(total * 2, 128)
 

time: 431 us -> 91.4 us (0.21)
  blocking collectives: 310 us -> 0 us
  Pallas kernels: 111 us -> 78 us
    all_gather x1 -> x0, blocking collectives: 310 us -> none  [on_device(): lax.all_gather(injection_level, ('gx', 'gy'), tiled=True)]
    pallas_call x1, Pallas kernels: 43.5 us -> 17.5 us  [gather(): pl.pallas_call(gather_kernel, out_shape=jax.ShapeDtypeStruct((ny, nx, 2,...]
    pallas_call x1, Pallas kernels: 50.1 us -> 42.1 us  [stencil(): pl.pallas_call(stencil_kernel, out_shape=(jax.ShapeDtypeStruct(f.shape, j...]
where the time goes in v1:
time: 91.4 us; the launch traced here: 91.1 us
  Pallas kernels  78 us (85%)
  local copies, waits for them, and re-layouts  8.53 us (9%)
  other arithmetic  3.61 us (4%)
    pallas_call x1, Pallas kernels, stencil(): pl.pallas_call(stencil_kernel, out_shape=(jax.ShapeDtypeStruct(f.shape, j...  42.1 us
    pallas_call x1, Pallas kernels, gather(): pl.pallas_call(gather_kernel, out_shape=jax.ShapeDtypeStruct((ny, nx, 2,...  17.5 us
    pallas_call x1, Pallas kernels, exchange(): pl.pallas_call(exchange_kernel, out_shape=jax.ShapeDtypeStruct((nx, ny, 2...  14.1 us
    unnamed x10, local copies, waits for them, and re-layouts  5.46 us
    pallas_call x1, Pallas kernels, gradient(): pl.pallas_call(gradient_kernel, grid=(fire // width,), out_shape=jax.Shap...  4.21 us

profile of v1, /device:TPU:1, one launch (start us, length us, event | category | flops | bytes accessed | tf_op | source)
XLA Modules:
  0.0 91.1 jit_solution(10584175874320446658)
XLA Ops:
  0.6 0.8 reshape.358.profile
  1.4 0.9 %sign_compare_fusion.2 = pred[32768]{0:T(1024)(128)(4,1)S(1)} fusion(s32[32768]{0:T(1024)} %param.12), kind=kLoop, calls=%fused_computation.27 | loop fusion | flops 65536 | bytes 163840 | tf_op jit(solution)/shard_map/jit(floor_divide)/ne | solution.py:547
  2.4 1.0 %broadcast_divide_fusion = (s32[32768]{0:T(1024)S(1)}, s32[32768]{0:T(1024)S(1)}) fusion(s32[32768]{0:T(1024)} %param.12), kind=kLoop, calls=%fused_computation.35 | loop fusion | flops 65536 | bytes 393216 | tf_op jit(solution)/shard_map/jit(floor_divide)/div | solution.py:547
  3.5 0.2 fusion.7
  3.7 0.9 convert_compare_fusion
  4.6 0.2 convert_reduce_fusion
  4.8 0.1 copy.26.where
  4.9 0.2 fusion
  5.2 0.0 copy-start.3
  5.2 0.0 copy-start.2
  5.2 42.1 %stencil.1 = (f32[16,192,384]{2,1,0:T(8,128)}, s32[16,8,2,128]{3,2,1,0:T(2,128)}) custom-call(f32[16,192,384]{2,1,0:T(8,128)} %f_hbm.1, bf16[16,192,384]{2,1,0:T(8,128)(2,1)} %cu_hbm.1, bf16[16,192,384]{2,1,0:T(8,128)(2,1)} %cv_hbm.1, bf16[16,192,384]{2,1,0:T(8,128)(2,1)} %k_hbm.1, s32[2,128]{1,0:T(2,128)} %bitcast.41), custom_call_target="tpu_custom_call" | custom-call | tf_op jit(solution)/shard_map/stencil/pallas_call | solution.py:319
  47.4 0.9 %copy.29 = s32[16,8,2,128]{3,1,2,0:T(8,128)S(1)} copy(s32[16,8,2,128]{3,2,1,0:T(2,128)} %get-tuple-element.5) | data formatting | bytes 262144
  48.3 0.0 copy-done.3
  48.3 0.3 select_reduce_fusion.1
  48.6 0.1 fusion.14
  48.7 0.9 copy.25
  49.6 1.2 %reshape.357.table = s32[2048]{0:T(1024)S(1)} reshape(s32[128,4,4]{2,1,0:T(4,128)} %copy.25) | data formatting | bytes 16384 | tf_op jit(solution)/shard_map/reshape | solution.py:596
  50.7 0.0 copy-start
  50.8 2.3 %copy-done = f32[16,192,384]{2,1,0:T(8,128)S(1)} copy-done((f32[16,192,384]{2,1,0:T(8,128)S(1)}, f32[16,192,384]{2,1,0:T(8,128)}, u32[]{:S(2)}) %copy-start) | copy-done | bytes 4718616
  53.1 17.5 %gather.1.rows = f32[8,16,2,128]{3,2,1,0:T(2,128)S(1)} custom-call(s32[2048]{0:T(1024)S(1)} %reshape.357.table, f32[256]{0:T(256)S(1)} %reshape.358.profile, f32[16,192,384]{2,1,0:T(8,128)S(1)} %copy-done), custom_call_target="tpu_custom_call" | custom-call | tf_op jit(solution)/shard_map/gather/pallas_call | solution.py:405
  70.6 14.1 %exchange.1 = f32[16,8,2,128]{3,2,1,0:T(2,128)S(1)} custom-call(f32[8,16,2,128]{3,2,1,0:T(2,128)S(1)} %gather.1.rows), custom_call_target="tpu_custom_call" | custom-call | tf_op jit(solution)/shard_map/exchange/pallas_call | solution.py:473
  84.7 0.0 copy-done.2
  84.7 0.0 copy-start.1
  84.7 4.2 %gradient.1 = bf16[256,6400]{1,0:T(8,128)(2,1)} custom-call(f32[256,128]{1,0:T(8,128)S(1)} %bitcast.36, s32[256,2]{1,0:T(8,128)S(1)} %copy.26.where, bf16[256,6400]{1,0:T(8,128)(2,1)S(1)} %copy-done.2), custom_call_target="tpu_custom_call" | custom-call | tf_op jit(solution)/shard_map/gradient/pallas_call | solution.py:530
  89.0 0.0 copy-done.1
  89.0 2.2 %copy.34 = f32[16,192,384]{2,1,0:T(8,128)} copy(f32[16,192,384]{2,1,0:T(8,128)S(1)} %copy-done.1) | data formatting | bytes 9437184
  (10 shorter events, 0.2 us)
Async XLA Ops:
  5.2 43.1 %copy-start.3 = (pred[128,256]{1,0:T(8,128)(4,1)S(1)}, pred[128,256]{1,0:T(8,128)(4,1)}, u32[]{:S(2)}) copy-start(pred[128,256]{1,0:T(8,128)(4,1)} %get-tuple-element.8) | copy-start | bytes 98308
  5.2 79.5 %copy-start.2 = (bf16[256,6400]{1,0:T(8,128)(2,1)S(1)}, bf16[256,6400]{1,0:T(8,128)(2,1)}, u32[]{:S(2)}) copy-start(bf16[256,6400]{1,0:T(8,128)(2,1)} %burn.1) | copy-start | bytes 9830404
  50.7 2.3 %copy-start = (f32[16,192,384]{2,1,0:T(8,128)S(1)}, f32[16,192,384]{2,1,0:T(8,128)}, u32[]{:S(2)}) copy-start(f32[16,192,384]{2,1,0:T(8,128)} %get-tuple-element.20.field) | copy-start | bytes 14155780
  84.7 4.2 %copy-start.1 = (f32[16,192,384]{2,1,0:T(8,128)S(1)}, f32[16,192,384]{2,1,0:T(8,128)}, u32[]{:S(2)}) copy-start(f32[16,192,384]{2,1,0:T(8,128)} %get-tuple-element.20.field) | copy-start | bytes 14155780

commit v2 on v1

--- a/solution.py
+++ b/solution.py
@@ -23,10 +23,11 @@
 
 
 def stencil_kernel(
-    f_hbm, cu_hbm, cv_hbm, k_hbm, own, out, shared,
-    field, cu, cv, mix, work, ysend, yrecv, held,
+    f_hbm, cu_hbm, cv_hbm, k_hbm, own, table, profile, out, arrived,
+    field, cu, cv, mix, work, ysend, yrecv, held, shared, level_of, weights,
+    blocks, sums, depart, transit, again,
     load_sem, save_sem, xs_sem, xr_sem, ys_sem, yr_sem,
-    send1, recv1, send2, recv2,
+    send1, recv1, send2, recv2, send3, recv3, send4, recv4, level_sem,
 ):
     levels, rows, cols = field.shape
     tiles = cols // 128
@@ -241,6 +242,9 @@
                     if mode == "last":
                         for l in range(levels):
                             field[l, pl.ds(at, 16), 128 * j : 128 * j + 128] = values[l]
+                            for h in range(2):
+                                block = (2 * i + h) * tiles + j
+                                blocks[block, l] = values[l][8 * h : 8 * h + 8]
                     else:
                         result = mixed(values, at, j)
                         for l in range(levels):
@@ -292,8 +296,102 @@
     for copy in late:
         copy.wait()
     fori(1, ITERS, lambda n: run(n, "middle"))
+    fori(1, nx, lambda o: share_x(o).wait_recv())
+    to_scalars = pltpu.make_async_copy(shared, level_of, level_sem)
+    to_scalars.start()
     run(ITERS, "last")
-    fori(1, nx, lambda o: share_x(o).wait_recv())
+
+    def spread(r):
+        for l in range(levels):
+            weights[r, l] = jnp.full((8, 128), profile[r * levels + l], jnp.float32)
+
+    fori(0, profile.shape[0] // levels, spread)
+    to_scalars.wait()
+
+    lane8 = lax.broadcasted_iota(jnp.int32, (8, 128), 1)
+
+    def weigh(p, quad):
+        for k in range(16):
+            at = 4 * (4 * ((4 * quad + k // 4) * ny + p) + k % 4)
+            block = table[at]
+            r = level_of[4 * quad + k // 4, p, table[at + 2], table[at + 3]]
+            terms = [weights[r, l] * blocks[block, l] for l in range(levels)]
+            while len(terms) > 1:
+                terms = [a + b for a, b in zip(terms[::2], terms[1::2])]
+            sums[quad, k] = jnp.where(lane8 // 8 == table[at + 1], terms[0], 0.0)
+
+    def settle(p):
+        lists = [[sums[quad, k] for k in range(16)] for quad in range(nx // 4)]
+        for bit in (8, 4, 2, 1):
+            low = (lane8 // 8 & bit) == 0
+            for quad, found in enumerate(lists):
+                folded = []
+                for a, b in zip(found[: len(found) // 2], found[len(found) // 2 :]):
+                    keep, swap = jnp.where(low, a, b), jnp.where(low, b, a)
+                    moved = pltpu.roll(swap, 8 * bit, 1)
+                    if bit < 8:
+                        moved = jnp.where(low, pltpu.roll(swap, 128 - 8 * bit, 1), moved)
+                    folded.append(keep + moved)
+                lists[quad] = folded
+        for quad, found in enumerate(lists):
+            depart[p, quad] = found[0]
+
+    def along_y(o):
+        to = lax.rem(gy + o, ny)
+        return pltpu.make_async_remote_copy(
+            src_ref=depart.at[to],
+            dst_ref=transit.at[gy],
+            send_sem=send3.at[o],
+            recv_sem=recv3.at[o],
+            device_id=(gx, to),
+            device_id_type=MESH,
+        )
+
+    def along_x(o):
+        to = lax.rem(gx + o, nx)
+        return pltpu.make_async_remote_copy(
+            src_ref=again.at[to],
+            dst_ref=arrived.at[gx],
+            send_sem=send4.at[o],
+            recv_sem=recv4.at[o],
+            device_id=(to, gy),
+            device_id_type=MESH,
+        )
+
+    def depart_to(o):
+        p = lax.rem(gy + o, ny)
+        fori(0, nx // 4, lambda quad: weigh(p, quad))
+        settle(p)
+
+        @pl.when(o < ny)
+        def _():
+            along_y(o).start()
+
+    fori(1, ny + 1, depart_to)
+    transit[gy] = depart[gy]
+    fori(1, ny, lambda o: along_y(o).wait_recv())
+
+    def pass_on(quad):
+        for u in range(4):
+            for h in range(again.shape[1]):
+                packed = None
+                for j in range(min(ny, 4)):
+                    moved = transit[4 * h + j, quad]
+                    if j != u:
+                        moved = pltpu.roll(moved, 32 * (j - u) % 128, 1)
+                    packed = moved if j == 0 else jnp.where(lane8 // 32 == j, moved, packed)
+                again[4 * quad + u, h] = packed
+            o = lax.rem(4 * quad + u + nx - gx, nx)
+
+            @pl.when(o > 0)
+            def _():
+                along_x(o).start()
+
+    fori(0, nx // 4, pass_on)
+    arrived[gx] = again[gx]
+    fori(1, nx, lambda o: along_x(o).wait_recv())
+    fori(1, ny, lambda o: along_y(o).wait_send())
+    fori(1, nx, lambda o: along_x(o).wait_send())
     fori(1, ny, lambda o: share_y(o).wait_send())
     fori(1, nx, lambda o: share_x(o).wait_send())
     for save in saves:
@@ -310,19 +408,21 @@
     fori(0, ITERS, all_sent)
 
 
-def stencil(f, cu, cv, k, own, nx, ny):
+def stencil(f, cu, cv, k, own, table, profile, nx, ny):
     levels, rows, cols = f.shape
     any_space = pl.BlockSpec(memory_space=pl.ANY)
     vmem = pl.BlockSpec(memory_space=pltpu.VMEM)
     tiles = cols // 128
     chunks = rows // 32
+    smem = pl.BlockSpec(memory_space=pltpu.SMEM)
+    halves = max(1, ny // 4)
     return pl.pallas_call(
         stencil_kernel,
         out_shape=(
             jax.ShapeDtypeStruct(f.shape, jnp.float32),
-            jax.ShapeDtypeStruct((nx, ny, *own.shape), jnp.int32),
+            jax.ShapeDtypeStruct((nx, halves, 8, 128), jnp.float32),
         ),
-        in_specs=[any_space] * 4 + [vmem],
+        in_specs=[any_space] * 4 + [vmem, smem, smem],
         out_specs=(any_space, vmem),
         scratch_shapes=[
             pltpu.VMEM(f.shape, jnp.float32),
@@ -333,6 +433,14 @@
             pltpu.VMEM((ITERS, chunks, 16, 128), jnp.float32),
             pltpu.VMEM((ITERS, 2, chunks, 16, 128), jnp.float32),
             pltpu.VMEM((ny, *own.shape), jnp.int32),
+            pltpu.VMEM((nx, ny, *own.shape), jnp.int32),
+            pltpu.SMEM((nx, ny, *own.shape), jnp.int32),
+            pltpu.VMEM((profile.shape[0] // levels, levels, 8, 128), jnp.float32),
+            pltpu.VMEM((rows // 8 * tiles, levels, 8, 128), jnp.float32),
+            pltpu.VMEM((nx // 4, 16, 8, 128), jnp.float32),
+            pltpu.VMEM((ny, nx // 4, 8, 128), jnp.float32),
+            pltpu.VMEM((ny, nx // 4, 8, 128), jnp.float32),
+            pltpu.VMEM((nx, halves, 8, 128), jnp.float32),
             pltpu.SemaphoreType.DMA((3, 4)),
             pltpu.SemaphoreType.DMA((4,)),
             pltpu.SemaphoreType.DMA((ITERS, 2)),
@@ -343,159 +451,44 @@
             pltpu.SemaphoreType.DMA((ny,)),
             pltpu.SemaphoreType.DMA((nx,)),
             pltpu.SemaphoreType.DMA((nx,)),
+            pltpu.SemaphoreType.DMA((ny,)),
+            pltpu.SemaphoreType.DMA((ny,)),
+            pltpu.SemaphoreType.DMA((nx,)),
+            pltpu.SemaphoreType.DMA((nx,)),
+            pltpu.SemaphoreType.DMA,
         ],
         compiler_params=pltpu.CompilerParams(
             collective_id=0, has_side_effects=True, vmem_limit_bytes=58 * MIB
         ),
         name="stencil",
-    )(f, cu, cv, k, own)
-
-
-def gather_kernel(table, profile, field, out, weights, sums):
-    levels = field.shape[0]
-    ny, nx = out.shape[0], out.shape[1]
-    lane = lax.broadcasted_iota(jnp.int32, (8, 128), 1)
-    sub = lax.broadcasted_iota(jnp.int32, (8, 128), 0)
-
-    def spread(r):
-        for l in range(levels):
-            weights[r, l] = jnp.full((8, 128), profile[r * levels + l], jnp.float32)
-
-    fori(0, profile.shape[0] // levels, spread)
-
-    def weigh(d):
-        for h in range(4):
-            q = 4 * (4 * d + h)
-            row = pl.multiple_of(table[q], 8)
-            col = pl.multiple_of(table[q + 1], 128)
-            r = table[q + 3]
-            terms = [
-                weights[r, l] * field[l, pl.ds(row, 8), pl.ds(col, 128)] for l in range(levels)
-            ]
-            while len(terms) > 1:
-                terms = [a + b for a, b in zip(terms[::2], terms[1::2])]
-            sums[4 * d + h] = terms[0]
-
-    fori(0, nx * ny, weigh)
-
-    def flatten(c):
-        d0 = lax.rem(c, nx // unroll) * unroll, c // (nx // unroll)
-        for u in range(unroll):
-            g, p = d0[0] + u, d0[1]
-            s0 = 4 * (g * ny + p)
-            for pair in range(2):
-                found = []
-                for h in range(2):
-                    s = s0 + 2 * pair + h
-                    found.append(pltpu.roll(sums[s], table[4 * s + 2], 1))
-                both = jnp.where(lane < 64, found[0], found[1])
-                for bit in (1, 2, 4):
-                    both = jnp.where(sub // bit % 2 == 1, pltpu.roll(both, 8 * bit, 1), both)
-                both = jnp.where(lane // 8 % 8 == sub, both, 0.0)
-                out[p, g, pair : pair + 1, :] = jnp.sum(both, axis=0, keepdims=True)
-
-    unroll = 4
-    fori(0, nx * ny // unroll, flatten)
-
-
-def gather(table, profile, field, nx, ny):
-    smem = pl.BlockSpec(memory_space=pltpu.SMEM)
-    vmem = pl.BlockSpec(memory_space=pltpu.VMEM)
-    levels = field.shape[0]
-    return pl.pallas_call(
-        gather_kernel,
-        out_shape=jax.ShapeDtypeStruct((ny, nx, 2, 128), jnp.float32),
-        in_specs=[smem, smem, vmem],
-        out_specs=vmem,
-        scratch_shapes=[
-            pltpu.VMEM((profile.shape[0] // levels, levels, 8, 128), jnp.float32),
-            pltpu.VMEM((4 * nx * ny, 8, 128), jnp.float32),
-        ],
-        compiler_params=pltpu.CompilerParams(vmem_limit_bytes=24 * MIB),
-        name="gather",
-    )(table, profile, field)
-
-
-def exchange_kernel(rows, out, held, send1, recv1, send2, recv2):
-    ny, nx = rows.shape[0], rows.shape[1]
-    gx, gy = lax.axis_index("gx"), lax.axis_index("gy")
-    barrier = pltpu.get_barrier_semaphore()
-
-    def greet_y(o):
-        pl.semaphore_signal(
-            barrier, inc=1, device_id=(gx, lax.rem(gy + o, ny)), device_id_type=MESH
-        )
-
-    def greet_x(o):
-        pl.semaphore_signal(
-            barrier, inc=1, device_id=(lax.rem(gx + o, nx), gy), device_id_type=MESH
-        )
-
-    fori(1, ny, greet_y)
-    fori(1, nx, greet_x)
-    pl.semaphore_wait(barrier, nx + ny - 2)
-
-    def first(o):
-        to = lax.rem(gy + o, ny)
-        return pltpu.make_async_remote_copy(
-            src_ref=rows.at[to],
-            dst_ref=held.at[gy],
-            send_sem=send1.at[o],
-            recv_sem=recv1.at[o],
-            device_id=(gx, to),
-            device_id_type=MESH,
-        )
-
-    def second(o):
-        to = lax.rem(gx + o, nx)
-        return pltpu.make_async_remote_copy(
-            src_ref=held.at[:, to],
-            dst_ref=out.at[gx],
-            send_sem=send2.at[o],
-            recv_sem=recv2.at[o],
-            device_id=(to, gy),
-            device_id_type=MESH,
-        )
-
-    fori(1, ny, lambda o: first(o).start())
-    held[gy] = rows[gy]
-    fori(1, ny, lambda o: first(o).wait_recv())
-    fori(1, nx, lambda o: second(o).start())
-    out[gx] = held[:, gx]
-    fori(1, nx, lambda o: second(o).wait_recv())
-    fori(1, ny, lambda o: first(o).wait_send())
-    fori(1, nx, lambda o: second(o).wait_send())
-
-
-def exchange(rows):
-    ny, nx = rows.shape[0], rows.shape[1]
-    vmem = pl.BlockSpec(memory_space=pltpu.VMEM)
-    return pl.pallas_call(
-        exchange_kernel,
-        out_shape=jax.ShapeDtypeStruct((nx, ny, 2, 128), jnp.float32),
-        in_specs=[vmem],
-        out_specs=vmem,
-        scratch_shapes=[
-            pltpu.VMEM(rows.shape, jnp.float32),
-            pltpu.SemaphoreType.DMA((ny,)),
-            pltpu.SemaphoreType.DMA((ny,)),
-            pltpu.SemaphoreType.DMA((nx,)),
-            pltpu.SemaphoreType.DMA((nx,)),
-        ],
-        compiler_params=pltpu.CompilerParams(
-            collective_id=1, has_side_effects=True, vmem_limit_bytes=16 * MIB
-        ),
-        name="exchange",
-    )(rows)
-
-
-def gradient_kernel(rows, where, burn, out, column):
+    )(f, cu, cv, k, own, table, profile)
+
+
+def gradient_kernel(rows, where, burn, state, out, state_out, column, held, copy_sem):
     step = pl.program_id(0)
+    part = state.shape[0] // 4
+    loads, saves = [], []
+    for i in range(4):
+        at = pl.ds(part * i, part)
+        loads.append(pltpu.make_async_copy(state.at[at], held.at[at], copy_sem.at[0, i]))
+        saves.append(pltpu.make_async_copy(held.at[at], state_out.at[at], copy_sem.at[1, i]))
     tiles_dev, width = burn.shape
 
     @pl.when(step == 0)
     def _():
+        for load in loads:
+            load.start()
         values = rows[...]
+        sub = lax.broadcasted_iota(jnp.int32, values.shape, 1)
+        group = lax.broadcasted_iota(jnp.int32, values.shape, 2) // 8
+        for bit in (1, 2, 4):
+            low = pltpu.roll(pltpu.roll(values, 8 - bit, 1), 8 * bit, 2)
+            high = pltpu.roll(pltpu.roll(values, bit, 1), 128 - 8 * bit, 2)
+            in_row, in_group = sub // bit % 2, group // bit % 2
+            values = jnp.where(
+                in_row == in_group, values, jnp.where(in_group == 1, low, high)
+            )
+        values = values.reshape(-1, 128)
         high = values.astype(jnp.bfloat16)
         rest = values - high.astype(jnp.float32)
         mid = rest.astype(jnp.bfloat16)
@@ -523,24 +516,46 @@
     expanded = jnp.dot(column[...], spread, preferred_element_type=jnp.float32)
     out[...] = (burn[...].astype(jnp.float32) * expanded).astype(jnp.bfloat16)
 
-
-def gradient(rows, where, burn):
+    for i in range(4):
+        @pl.when(step == i)
+        def _():
+            loads[i].wait()
+            saves[i].start()
+
+    @pl.when(step == pl.num_programs(0) - 1)
+    def _():
+        for save in saves:
+            save.wait()
+
+
+def gradient(rows, where, burn, state):
     tiles_dev, fire = burn.shape
     width = 1280
     return pl.pallas_call(
         gradient_kernel,
         grid=(fire // width,),
-        out_shape=jax.ShapeDtypeStruct(burn.shape, jnp.bfloat16),
+        out_shape=(
+            jax.ShapeDtypeStruct(burn.shape, jnp.bfloat16),
+            jax.ShapeDtypeStruct(state.shape, state.dtype),
+        ),
         in_specs=[
-            pl.BlockSpec(rows.shape, lambda s: (0, 0)),
+            pl.BlockSpec(rows.shape, lambda s: (0, 0, 0)),
             pl.BlockSpec(where.shape, lambda s: (0, 0)),
             pl.BlockSpec((tiles_dev, width), lambda s: (0, s)),
+            pl.BlockSpec(memory_space=pl.ANY),
         ],
-        out_specs=pl.BlockSpec((tiles_dev, width), lambda s: (0, s)),
-        scratch_shapes=[pltpu.VMEM((tiles_dev, 256), jnp.bfloat16)],
-        compiler_params=pltpu.CompilerParams(vmem_limit_bytes=24 * MIB),
+        out_specs=(
+            pl.BlockSpec((tiles_dev, width), lambda s: (0, s)),
+            pl.BlockSpec(memory_space=pl.ANY),
+        ),
+        scratch_shapes=[
+            pltpu.VMEM((tiles_dev, 256), jnp.bfloat16),
+            pltpu.VMEM(state.shape, state.dtype),
+            pltpu.SemaphoreType.DMA((2, 4)),
+        ],
+        compiler_params=pltpu.CompilerParams(vmem_limit_bytes=50 * MIB),
         name="gradient",
-    )(rows, where, burn)
+    )(rows, where, burn, state)
 
 
 def locate(block_ids, per_x, per_y, blocks_y, gy_count):
@@ -583,26 +598,35 @@
     local = jnp.sum(jnp.where(hits, local_block[:, None, :], 0), axis=2)
     block_row = local // per_y
     lane_at = local % per_y * TB
-    shift = (64 * (slots % 2)[None, :] - lane_at) % 128
-
-    state_field, all_levels = stencil(
+    place = jnp.sum(jnp.where(hits, jnp.arange(tiles_dev, dtype=jnp.int32), 0), axis=2)
+    share = min(tiles_dev, 128)
+    table = jnp.stack(
+        [
+            block_row * (width_y // 128) + lane_at // 128,
+            lane_at % 128 // TB,
+            place // share,
+            place % share,
+        ],
+        axis=2,
+    ).reshape(-1)
+
+    state_field, rows = stencil(
         adjoint_forcing, courant_x, courant_y, vertical_mix,
-        injection_level.reshape(-1, min(tiles_dev, 128)), gx_count, gy_count,
+        injection_level.reshape(-1, share), table, plume_profile.reshape(-1),
+        gx_count, gy_count,
     )
-    all_levels = all_levels.reshape(total, tiles_dev)
-    level = jnp.sum(jnp.where(hits, all_levels[:, None, :], 0), axis=2)
-    table = jnp.stack(
-        [block_row * TB, lane_at // 128 * 128, shift, level], axis=2
-    ).reshape(-1)
-    rows = gather(table, plume_profile.reshape(-1), state_field, gx_count, gy_count)
-    rows = exchange(rows).reshape(total * 2, 128)
+    rows = rows.reshape(-1, 8, 128)
 
     own = lax.dynamic_slice_in_dim(source, me, 1, 0).reshape(tiles_dev)
     positions = jnp.arange(tiles_dev, dtype=jnp.int32)
     earlier = (own[None, :] == own[:, None]) & (positions[None, :] <= positions[:, None])
     arrival = jnp.sum(earlier.astype(jnp.int32), axis=1) - 1
-    where = jnp.stack([own * 2 + arrival // 2, arrival % 2], axis=1)
-    return (state_field, gradient(rows, where, burn_weight))
+    far, near = own // gy_count, own % gy_count
+    spot = near % 4 * 4 + arrival
+    row = (far * max(1, gy_count // 4) + near // 4) * 8 + spot % 8
+    where = jnp.stack([row, spot // 8], axis=1)
+    gradient_out, state_out = gradient(rows, where, burn_weight, state_field)
+    return (state_out, gradient_out)
 
 
 def solution(mesh):

time: 91.4 us -> 68.6 us (0.75)
  Pallas kernels: 78 us -> 60.9 us
  local copies, waits for them, and re-layouts: 8.53 us -> 3.52 us
    pallas_call x3 -> x1, Pallas kernels: 35.8 us -> 5.54 us  [gradient(): pl.pallas_call(gradient_kernel, grid=(fire // width,), out_shape=(jax.Sha...]
    pallas_call x1, Pallas kernels: 42.1 us -> 55.4 us  [stencil(): pl.pallas_call(stencil_kernel, out_shape=(jax.ShapeDtypeStruct(f.shape, j...]
    unnamed x10 -> x4, local copies, waits for them, and re-layouts: 5.46 us -> 0.9 us
where the time goes in v2:
time: 68.6 us; the launch traced here: 68.4 us
  Pallas kernels  60.9 us (89%)
  local copies, waits for them, and re-layouts  3.52 us (5%)
  other arithmetic  2.96 us (4%)
  between operations  0.76 us (1%)
    pallas_call x1, Pallas kernels, stencil(): pl.pallas_call(stencil_kernel, out_shape=(jax.ShapeDtypeStruct(f.shape, j...  55.4 us
    pallas_call x1, Pallas kernels, gradient(): pl.pallas_call(gradient_kernel, grid=(fire // width,), out_shape=(jax.Sha...  5.54 us

profile of v2, /device:TPU:1, one launch (start us, length us, event | category | flops | bytes accessed | tf_op | source)
XLA Modules:
  0.0 68.4 jit_solution(11121149020581601955)
XLA Ops:
  0.6 1.3 %reshape.597.profile = f32[256]{0:T(256)} reshape(f32[16,16]{1,0:T(8,128)} %param.14) | data formatting | bytes 2048 | tf_op jit(solution)/shard_map/reshape | solution.py:615
  2.0 0.9 %sign_compare_fusion.2 = pred[32768]{0:T(1024)(128)(4,1)S(1)} fusion(s32[32768]{0:T(1024)} %param.12), kind=kLoop, calls=%fused_computation.26 | loop fusion | flops 65536 | bytes 163840 | tf_op jit(solution)/shard_map/jit(floor_divide)/ne | solution.py:562
  3.0 1.0 %broadcast_divide_fusion = (s32[32768]{0:T(1024)S(1)}, s32[32768]{0:T(1024)S(1)}) fusion(s32[32768]{0:T(1024)} %param.12), kind=kLoop, calls=%fused_computation.34 | loop fusion | flops 65536 | bytes 393216 | tf_op jit(solution)/shard_map/jit(floor_divide)/div | solution.py:562
  4.0 0.2 fusion.7
  4.2 0.3 convert_compare_fusion
  4.5 0.2 convert_reduce_fusion
  4.8 0.1 copy.36.where
  4.9 0.2 fusion
  5.2 0.3 select_reduce_fusion.1
  5.5 0.2 copy.35
  5.7 0.9 %reshape.596.table = s32[2048]{0:T(1024)} reshape(s32[128,4,4]{2,1,0:T(4,128)S(1)} %copy.35) | data formatting | bytes 16384 | tf_op jit(solution)/shard_map/reshape | solution.py:611
  6.6 0.0 copy-start
  6.6 55.4 %stencil.1 = (f32[16,192,384]{2,1,0:T(8,128)}, f32[16,2,8,128]{3,2,1,0:T(8,128)}) custom-call(f32[16,192,384]{2,1,0:T(8,128)} %f_hbm.1, bf16[16,192,384]{2,1,0:T(8,128)(2,1)} %cu_hbm.1, bf16[16,192,384]{2,1,0:T(8,128)(2,1)} %cv_hbm.1, bf16[16,192,384]{2,1,0:T(8,128)(2,1)} %k_hbm.1, s32[2,128]{1,0:T(2,128)} %bitcast.74, s32[2048]{0:T(1024)} %reshape.596.table, ...), custom_call_target="tpu_custom_call" | custom-call | tf_op jit(solution)/shard_map/stencil/pallas_call | solution.py:419
  62.0 0.0 copy-done
  62.0 0.0 copy-start.1
  62.0 0.9 %copy-done.1 = f32[16,2,8,128]{3,2,1,0:T(8,128)S(1)} copy-done((f32[16,2,8,128]{3,2,1,0:T(8,128)S(1)}, f32[16,2,8,128]{3,2,1,0:T(8,128)}, u32[]{:S(2)}) %copy-start.1) | copy-done | bytes 131096
  62.9 5.5 %gradient.1 = (bf16[256,6400]{1,0:T(8,128)(2,1)}, f32[16,192,384]{2,1,0:T(8,128)}) custom-call(f32[32,8,128]{2,1,0:T(8,128)S(1)} %bitcast.71, s32[256,2]{1,0:T(8,128)S(1)} %copy.36.where, bf16[256,6400]{1,0:T(8,128)(2,1)S(1)} %copy-done, f32[16,192,384]{2,1,0:T(8,128)} %get-tuple-element.7.state), custom_call_target="tpu_custom_call" | custom-call | tf_op jit(solution)/shard_map/gradient/pallas_call | solution.py:534
  (11 shorter events, 0.2 us)
Async XLA Ops:
  6.6 55.4 %copy-start = (bf16[256,6400]{1,0:T(8,128)(2,1)S(1)}, bf16[256,6400]{1,0:T(8,128)(2,1)}, u32[]{:S(2)}) copy-start(bf16[256,6400]{1,0:T(8,128)(2,1)} %burn.1) | copy-start | bytes 9830404
  62.0 0.9 %copy-start.1 = (f32[16,2,8,128]{3,2,1,0:T(8,128)S(1)}, f32[16,2,8,128]{3,2,1,0:T(8,128)}, u32[]{:S(2)}) copy-start(f32[16,2,8,128]{3,2,1,0:T(8,128)} %get-tuple-element.6) | copy-start | bytes 393220

commit v3 on v2

--- a/solution.py
+++ b/solution.py
@@ -24,7 +24,7 @@
 
 def stencil_kernel(
     f_hbm, cu_hbm, cv_hbm, k_hbm, own, table, profile, out, arrived,
-    field, cu, cv, mix, work, ysend, yrecv, held, shared, level_of, weights,
+    field, cu, cv, mix, work0, work1, ysend, yrecv, held, shared, level_of, weights,
     blocks, sums, depart, transit, again,
     load_sem, save_sem, xs_sem, xr_sem, ys_sem, yr_sem,
     send1, recv1, send2, recv2, send3, recv3, send4, recv4, level_sem,
@@ -32,8 +32,8 @@
     levels, rows, cols = field.shape
     tiles = cols // 128
     groups = rows // 16
-    chunks = groups // 2
-    early = max(1, (chunks - 1) // 2)
+    chunks = groups // 4
+    work = (work0, work1)
     gx, gy = lax.axis_index("gx"), lax.axis_index("gy")
     nx, ny = lax.axis_size("gx"), lax.axis_size("gy")
     have_x = (gx > 0, gx < nx - 1)
@@ -43,10 +43,9 @@
     lane = lax.broadcasted_iota(jnp.int32, (16, 128), 1)
     odd = lane % 2 == 1
 
-    pieces = [(0, 16, 0), (rows - 16, 16, 0), (16, 32 * early, 1)]
-    if chunks - 1 > early:
-        pieces.append((16 + 32 * early, 32 * (chunks - 1 - early), 1 + early))
-    bounds = sorted({first for _, _, first in pieces}) + [chunks]
+    pieces = [(0, 48, 0), (rows - 16, 16, 0)]
+    pieces += [(64 * c - 16, 64, c) for c in range(1, chunks)]
+    bounds = list(range(chunks + 1))
 
     def parts_copy(src, dst, sem):
         return [
@@ -74,8 +73,8 @@
     def clear(l):
         for b in range(2):
             for j in range(tiles):
-                work[b, l, j, 7:8, :] = zero_row
-                work[b, l, j, rows + 8 : rows + 9, :] = zero_row
+                work[b][l, j, 7:8, :] = zero_row
+                work[b][l, j, rows + 8 : rows + 9, :] = zero_row
 
     fori(0, levels, clear)
     yrecv[...] = jnp.zeros_like(yrecv)
@@ -120,11 +119,11 @@
     held[gy] = own[...]
 
     def x_copy(n, side):
-        b = lax.rem(n, 2)
+        b = n % 2
         src, dst = ((8, rows + 8), (rows + 7, 7))[side]
         return pltpu.make_async_remote_copy(
-            src_ref=work.at[b, :, :, pl.ds(src, 1), :],
-            dst_ref=work.at[b, :, :, pl.ds(dst, 1), :],
+            src_ref=work[b].at[:, :, pl.ds(src, 1), :],
+            dst_ref=work[b].at[:, :, pl.ds(dst, 1), :],
             send_sem=xs_sem.at[n, side],
             recv_sem=xr_sem.at[n, side],
             device_id=peer_x[side],
@@ -199,11 +198,11 @@
     def moved_by_wind(b, at, here, j, halo):
         values = []
         for l in range(levels):
-            c = work[b, l, j, pl.ds(here, 16), :]
-            up = work[b, l, j, pl.ds(here + 1, 16), :]
-            down = work[b, l, j, pl.ds(here - 1, 16), :]
-            left = halo[l] if j == 0 else work[b, l, j - 1, pl.ds(here, 16), :]
-            right = halo[l] if j == tiles - 1 else work[b, l, j + 1, pl.ds(here, 16), :]
+            c = work[b][l, j, pl.ds(here, 16), :]
+            up = work[b][l, j, pl.ds(here + 1, 16), :]
+            down = work[b][l, j, pl.ds(here - 1, 16), :]
+            left = halo[l] if j == 0 else work[b][l, j - 1, pl.ds(here, 16), :]
+            right = halo[l] if j == tiles - 1 else work[b][l, j + 1, pl.ds(here, 16), :]
             left = pltpu.roll(jnp.where(lane == 127, left, c), 1, 1)
             right = pltpu.roll(jnp.where(lane == 0, right, c), 127, 1)
             su = cu[l, pl.ds(at, 16), 128 * j : 128 * j + 128].astype(jnp.float32)
@@ -214,14 +213,14 @@
         return values
 
     def run(n, mode):
-        source, target = lax.rem(n + 1, 2), lax.rem(n, 2)
+        source, target = (n + 1) % 2, n % 2
 
         def chunk_of(chunk):
             if mode != "first":
                 await_y(n - 1, chunk)
             packed = []
-            for m in range(2):
-                i = jnp.where(chunk == 0, m * (groups - 1), 2 * chunk - 1 + m)
+            for m in range(4):
+                i = jnp.where(chunk == 0, (0, groups - 1, 1, 2)[m], 4 * chunk - 1 + m)
                 at = pl.multiple_of(16 * i, 16)
                 here = pl.multiple_of(8 + 16 * i, 8)
                 if mode != "first":
@@ -248,15 +247,18 @@
                     else:
                         result = mixed(values, at, j)
                         for l in range(levels):
-                            work[target, l, j, pl.ds(here, 16), :] = result[l]
+                            work[target][l, j, pl.ds(here, 16), :] = result[l]
                 if mode != "last":
                     ends = [
-                        [work[target, l, j, pl.ds(here, 16), :] for l in range(levels)]
+                        [work[target][l, j, pl.ds(here, 16), :] for l in range(levels)]
                         for j in (0, tiles - 1)
                     ]
                     packed.append(pack(ends[0], ends[1], m))
             if mode != "last":
-                ysend[n, chunk] = jnp.where((lane >= 31) & (lane < 63), packed[1], packed[0])
+                ends = packed[0]
+                for m in range(1, 4):
+                    ends = jnp.where((lane >= 32 * m - 1) & (lane < 32 * m + 31), packed[m], ends)
+                ysend[n, chunk] = ends
                 send_y(n, chunk)
 
         def edges_first(chunk):
@@ -264,10 +266,8 @@
             def _():
                 if mode != "first":
                     await_x(n - 1)
-                if mode == "middle":
-                    @pl.when(n >= 2)
-                    def _():
-                        await_x_sent(n - 2)
+                if mode == "middle" and n >= 2:
+                    await_x_sent(n - 2)
 
             chunk_of(chunk)
             if mode != "last":
@@ -295,7 +295,8 @@
     shared[gx] = held[...]
     for copy in late:
         copy.wait()
-    fori(1, ITERS, lambda n: run(n, "middle"))
+    for n in range(1, ITERS):
+        run(n, "middle")
     fori(1, nx, lambda o: share_x(o).wait_recv())
     to_scalars = pltpu.make_async_copy(shared, level_of, level_sem)
     to_scalars.start()
@@ -303,22 +304,22 @@
 
     def spread(r):
         for l in range(levels):
-            weights[r, l] = jnp.full((8, 128), profile[r * levels + l], jnp.float32)
-
-    fori(0, profile.shape[0] // levels, spread)
+            weights[r, l] = jnp.full((8, 128), profile[r, l], jnp.float32)
+
+    fori(0, profile.shape[0], spread)
     to_scalars.wait()
 
     lane8 = lax.broadcasted_iota(jnp.int32, (8, 128), 1)
 
     def weigh(p, quad):
         for k in range(16):
-            at = 4 * (4 * ((4 * quad + k // 4) * ny + p) + k % 4)
-            block = table[at]
-            r = level_of[4 * quad + k // 4, p, table[at + 2], table[at + 3]]
+            g = 4 * quad + k // 4
+            block, lanes, high, low = (table[4 * a + k % 4, g * ny + p] for a in range(4))
+            r = level_of[g, p, high, low]
             terms = [weights[r, l] * blocks[block, l] for l in range(levels)]
             while len(terms) > 1:
                 terms = [a + b for a, b in zip(terms[::2], terms[1::2])]
-            sums[quad, k] = jnp.where(lane8 // 8 == table[at + 1], terms[0], 0.0)
+            sums[quad, k] = jnp.where(lane8 // 8 == lanes, terms[0], 0.0)
 
     def settle(p):
         lists = [[sums[quad, k] for k in range(16)] for quad in range(nx // 4)]
@@ -413,7 +414,7 @@
     any_space = pl.BlockSpec(memory_space=pl.ANY)
     vmem = pl.BlockSpec(memory_space=pltpu.VMEM)
     tiles = cols // 128
-    chunks = rows // 32
+    chunks = rows // 64
     smem = pl.BlockSpec(memory_space=pltpu.SMEM)
     halves = max(1, ny // 4)
     return pl.pallas_call(
@@ -429,13 +430,14 @@
             pltpu.VMEM(f.shape, jnp.bfloat16),
             pltpu.VMEM(f.shape, jnp.bfloat16),
             pltpu.VMEM(f.shape, jnp.bfloat16),
-            pltpu.VMEM((2, levels, tiles, rows + 16, 128), jnp.float32),
+            pltpu.VMEM((levels, tiles, rows + 16, 128), jnp.float32),
+            pltpu.VMEM((levels, tiles, rows + 16, 128), jnp.float32),
             pltpu.VMEM((ITERS, chunks, 16, 128), jnp.float32),
             pltpu.VMEM((ITERS, 2, chunks, 16, 128), jnp.float32),
             pltpu.VMEM((ny, *own.shape), jnp.int32),
             pltpu.VMEM((nx, ny, *own.shape), jnp.int32),
             pltpu.SMEM((nx, ny, *own.shape), jnp.int32),
-            pltpu.VMEM((profile.shape[0] // levels, levels, 8, 128), jnp.float32),
+            pltpu.VMEM((*profile.shape, 8, 128), jnp.float32),
             pltpu.VMEM((rows // 8 * tiles, levels, 8, 128), jnp.float32),
             pltpu.VMEM((nx // 4, 16, 8, 128), jnp.float32),
             pltpu.VMEM((ny, nx // 4, 8, 128), jnp.float32),
@@ -558,12 +560,16 @@
     )(rows, where, burn, state)
 
 
+def divide(values, by):
+    quotient = jnp.floor((values.astype(jnp.float32) + 0.5) * (1.0 / by)).astype(jnp.int32)
+    return quotient, values - quotient * by
+
+
 def locate(block_ids, per_x, per_y, blocks_y, gy_count):
-    block_row = block_ids // blocks_y
-    block_col = block_ids % blocks_y
-    source = block_row // per_x * gy_count + block_col // per_y
-    local_block = block_row % per_x * per_y + block_col % per_y
-    return (source, local_block)
+    block_row, block_col = divide(block_ids, blocks_y)
+    device_x, local_x = divide(block_row, per_x)
+    device_y, local_y = divide(block_col, per_y)
+    return device_x * gy_count + device_y, local_x * per_y + local_y
 
 
 def on_device(
@@ -596,23 +602,23 @@
     slots = jnp.arange(capacity, dtype=jnp.int32)
     hits = (is_mine[:, None, :] == 1) & (rank[:, None, :] == slots[None, :, None])
     local = jnp.sum(jnp.where(hits, local_block[:, None, :], 0), axis=2)
-    block_row = local // per_y
-    lane_at = local % per_y * TB
+    block_row, lane_at = divide(local, per_y)
+    lane_at = lane_at * TB
     place = jnp.sum(jnp.where(hits, jnp.arange(tiles_dev, dtype=jnp.int32), 0), axis=2)
     share = min(tiles_dev, 128)
-    table = jnp.stack(
+    table = jnp.concatenate(
         [
-            block_row * (width_y // 128) + lane_at // 128,
-            lane_at % 128 // TB,
-            place // share,
-            place % share,
+            (block_row * (width_y // 128) + lane_at // 128).T,
+            (lane_at % 128 // TB).T,
+            (place // share).T,
+            (place % share).T,
         ],
-        axis=2,
-    ).reshape(-1)
+        axis=0,
+    )
 
     state_field, rows = stencil(
         adjoint_forcing, courant_x, courant_y, vertical_mix,
-        injection_level.reshape(-1, share), table, plume_profile.reshape(-1),
+        injection_level.reshape(-1, share), table, plume_profile,
         gx_count, gy_count,
     )
     rows = rows.reshape(-1, 8, 128)

time: 68.6 us -> 63.1 us (0.920)
  Pallas kernels: 60.9 us -> 58.6 us
  local copies, waits for them, and re-layouts: 3.52 us -> 1.98 us
  other arithmetic: 2.96 us -> 1.44 us
    pallas_call x1, Pallas kernels: 55.4 us -> 53.1 us  [stencil(): pl.pallas_call(stencil_kernel, out_shape=(jax.ShapeDtypeStruct(f.shape, j...]
    reshape x2 -> x1, local copies, waits for them, and re-layouts: 2.2 us -> 0.95 us  [on_device(): slot_table = tile_block.reshape(total, tiles_dev)]
    div x1 -> x0, other arithmetic: 0.96 us -> none  [locate(): block_row = block_ids // blocks_y]
    ne x1 -> x0, other arithmetic: 0.94 us -> none  [locate(): block_row = block_ids // blocks_y]
where the time goes in v3:
time: 63.1 us; the launch traced here: 63 us
  Pallas kernels  58.6 us (93%)
  local copies, waits for them, and re-layouts  1.98 us (3%)
  other arithmetic  1.44 us (2%)
  between operations  0.73 us (1%)
    pallas_call x1, Pallas kernels, stencil(): pl.pallas_call(stencil_kernel, out_shape=(jax.ShapeDtypeStruct(f.shape, j...  53.1 us
    pallas_call x1, Pallas kernels, gradient(): pl.pallas_call(gradient_kernel, grid=(fire // width,), out_shape=(jax.Sha...  5.54 us

profile of v3, /device:TPU:1, one launch (start us, length us, event | category | flops | bytes accessed | tf_op | source)
XLA Modules:
  0.0 63.0 jit_solution(9185990482650476759)
XLA Ops:
  0.6 0.9 %reshape.324 = s32[128,256]{1,0:T(8,128)S(1)} reshape(s32[32768]{0:T(1024)} %param.12) | data formatting | bytes 262144 | tf_op jit(solution)/shard_map/reshape | solution.py:595
  1.6 0.1 subtract_add_fusion
  1.7 0.1 convert_compare_fusion
  1.9 0.2 convert_reduce_fusion
  2.1 0.1 copy.16.where
  2.3 0.2 fusion
  2.5 0.3 select_reduce_fusion.1
  2.9 0.6 pad_add_fusion.table
  3.5 0.0 copy-start
  3.5 53.1 %stencil.1 = (f32[16,192,384]{2,1,0:T(8,128)}, f32[16,2,8,128]{3,2,1,0:T(8,128)}) custom-call(f32[16,192,384]{2,1,0:T(8,128)} %f_hbm.1, bf16[16,192,384]{2,1,0:T(8,128)(2,1)} %cu_hbm.1, bf16[16,192,384]{2,1,0:T(8,128)(2,1)} %cv_hbm.1, bf16[16,192,384]{2,1,0:T(8,128)(2,1)} %k_hbm.1, s32[2,128]{1,0:T(2,128)} %bitcast.71, s32[16,128]{1,0:T(8,128)} %pad_add_fusion.table, ...), custom_call_target="tpu_custom_call" | custom-call | tf_op jit(solution)/shard_map/stencil/pallas_call | solution.py:420
  56.5 0.0 copy-done
  56.5 0.0 copy-start.1
  56.6 0.9 %copy-done.1 = f32[16,2,8,128]{3,2,1,0:T(8,128)S(1)} copy-done((f32[16,2,8,128]{3,2,1,0:T(8,128)S(1)}, f32[16,2,8,128]{3,2,1,0:T(8,128)}, u32[]{:S(2)}) %copy-start.1) | copy-done | bytes 131096
  57.5 5.5 %gradient.1 = (bf16[256,6400]{1,0:T(8,128)(2,1)}, f32[16,192,384]{2,1,0:T(8,128)}) custom-call(f32[32,8,128]{2,1,0:T(8,128)S(1)} %bitcast.68, s32[256,2]{1,0:T(8,128)S(1)} %copy.16.where, bf16[256,6400]{1,0:T(8,128)(2,1)S(1)} %copy-done, f32[16,192,384]{2,1,0:T(8,128)} %get-tuple-element.7.state), custom_call_target="tpu_custom_call" | custom-call | tf_op jit(solution)/shard_map/gradient/pallas_call | solution.py:536
  (7 shorter events, 0.1 us)
Async XLA Ops:
  3.5 53.1 %copy-start = (bf16[256,6400]{1,0:T(8,128)(2,1)S(1)}, bf16[256,6400]{1,0:T(8,128)(2,1)}, u32[]{:S(2)}) copy-start(bf16[256,6400]{1,0:T(8,128)(2,1)} %burn.1) | copy-start | bytes 9830404
  56.5 0.9 %copy-start.1 = (f32[16,2,8,128]{3,2,1,0:T(8,128)S(1)}, f32[16,2,8,128]{3,2,1,0:T(8,128)}, u32[]{:S(2)}) copy-start(f32[16,2,8,128]{3,2,1,0:T(8,128)} %get-tuple-element.6) | copy-start | bytes 393220

commit v4 on v3

--- a/solution.py
+++ b/solution.py
@@ -93,7 +93,6 @@
 
     fori(1, ny, greet_y)
     fori(1, nx, greet_x)
-    pl.semaphore_wait(barrier, nx + ny - 2)
 
     def share_y(o):
         return pltpu.make_async_remote_copy(
@@ -115,8 +114,11 @@
             device_id_type=MESH,
         )
 
-    fori(1, ny, lambda o: share_y(o).start())
     held[gy] = own[...]
+
+    def enter():
+        pl.semaphore_wait(barrier, nx + ny - 2)
+        fori(1, ny, lambda o: share_y(o).start())
 
     def x_copy(n, side):
         b = n % 2
@@ -254,6 +256,10 @@
                         for j in (0, tiles - 1)
                     ]
                     packed.append(pack(ends[0], ends[1], m))
+            if mode == "first":
+                @pl.when(chunk == 0)
+                def _():
+                    enter()
             if mode != "last":
                 ends = packed[0]
                 for m in range(1, 4):
@@ -361,7 +367,8 @@
 
     def depart_to(o):
         p = lax.rem(gy + o, ny)
-        fori(0, nx // 4, lambda quad: weigh(p, quad))
+        for quad in range(nx // 4):
+            weigh(p, quad)
         settle(p)
 
         @pl.when(o < ny)
@@ -388,15 +395,10 @@
             def _():
                 along_x(o).start()
 
-    fori(0, nx // 4, pass_on)
+    quads = nx // 4
+    fori(0, quads, lambda quad: pass_on(lax.rem(quad + gx // 4, quads)))
     arrived[gx] = again[gx]
-    fori(1, nx, lambda o: along_x(o).wait_recv())
-    fori(1, ny, lambda o: along_y(o).wait_send())
-    fori(1, nx, lambda o: along_x(o).wait_send())
-    fori(1, ny, lambda o: share_y(o).wait_send())
-    fori(1, nx, lambda o: share_x(o).wait_send())
-    for save in saves:
-        save.wait()
+
     for n in (ITERS - 2, ITERS - 1):
         await_x_sent(n)
 
@@ -404,9 +406,18 @@
         for side in range(2):
             @pl.when(have_y[side])
             def _():
-                fori(0, chunks, lambda chunk: y_copy(n, side, chunk).wait_send())
-
-    fori(0, ITERS, all_sent)
+                for chunk in range(chunks):
+                    y_copy(n, side, chunk).wait_send()
+
+    for n in range(ITERS):
+        all_sent(n)
+    fori(1, ny, lambda o: share_y(o).wait_send())
+    fori(1, nx, lambda o: share_x(o).wait_send())
+    fori(1, ny, lambda o: along_y(o).wait_send())
+    for save in saves:
+        save.wait()
+    fori(1, nx, lambda o: along_x(o).wait_recv())
+    fori(1, nx, lambda o: along_x(o).wait_send())
 
 
 def stencil(f, cu, cv, k, own, table, profile, nx, ny):
@@ -511,18 +522,18 @@
         )
         column[:, 128:256] = jnp.where(lane < 64, parts[2], 0.0).astype(jnp.bfloat16)
 
+    for i in range(4):
+        @pl.when(step == i)
+        def _():
+            loads[i].wait()
+            saves[i].start()
+
     cell = step * width + lax.broadcasted_iota(jnp.int32, (64, width), 1)
     start = SUB * lax.broadcasted_iota(jnp.int32, (64, width), 0)
     spread = ((cell >= start) & (cell < start + SUB)).astype(jnp.float32).astype(jnp.bfloat16)
     spread = jnp.concatenate([spread] * 4, axis=0)
     expanded = jnp.dot(column[...], spread, preferred_element_type=jnp.float32)
     out[...] = (burn[...].astype(jnp.float32) * expanded).astype(jnp.bfloat16)
-
-    for i in range(4):
-        @pl.when(step == i)
-        def _():
-            loads[i].wait()
-            saves[i].start()
 
     @pl.when(step == pl.num_programs(0) - 1)
     def _():

time: 63.1 us -> 62.1 us (0.984)
  Pallas kernels: 58.6 us -> 57.6 us
    pallas_call x1, Pallas kernels: 53.1 us -> 52.4 us  [stencil(): pl.pallas_call(stencil_kernel, out_shape=(jax.ShapeDtypeStruct(f.shape, j...]
where the time goes in v4:
time: 62.1 us; the launch traced here: 62 us
  Pallas kernels  57.6 us (93%)
  local copies, waits for them, and re-layouts  1.98 us (3%)
  other arithmetic  1.44 us (2%)
  between operations  0.73 us (1%)
    pallas_call x1, Pallas kernels, stencil(): pl.pallas_call(stencil_kernel, out_shape=(jax.ShapeDtypeStruct(f.shape, j...  52.4 us
    pallas_call x1, Pallas kernels, gradient(): pl.pallas_call(gradient_kernel, grid=(fire // width,), out_shape=(jax.Sha...  5.18 us

profile of v4, /device:TPU:1, one launch (start us, length us, event | category | flops | bytes accessed | tf_op | source)
XLA Modules:
  0.0 62.0 jit_solution(2211598038965570583)
XLA Ops:
  0.6 0.9 %reshape.324 = s32[128,256]{1,0:T(8,128)S(1)} reshape(s32[32768]{0:T(1024)} %param.12) | data formatting | bytes 262144 | tf_op jit(solution)/shard_map/reshape | solution.py:606
  1.6 0.1 subtract_add_fusion
  1.7 0.1 convert_compare_fusion
  1.9 0.2 convert_reduce_fusion
  2.1 0.1 copy.16.where
  2.3 0.2 fusion
  2.5 0.3 select_reduce_fusion.1
  2.9 0.6 pad_add_fusion.table
  3.5 0.0 copy-start
  3.5 52.4 %stencil.1 = (f32[16,192,384]{2,1,0:T(8,128)}, f32[16,2,8,128]{3,2,1,0:T(8,128)}) custom-call(f32[16,192,384]{2,1,0:T(8,128)} %f_hbm.1, bf16[16,192,384]{2,1,0:T(8,128)(2,1)} %cu_hbm.1, bf16[16,192,384]{2,1,0:T(8,128)(2,1)} %cv_hbm.1, bf16[16,192,384]{2,1,0:T(8,128)(2,1)} %k_hbm.1, s32[2,128]{1,0:T(2,128)} %bitcast.71, s32[16,128]{1,0:T(8,128)} %pad_add_fusion.table, ...), custom_call_target="tpu_custom_call" | custom-call | tf_op jit(solution)/shard_map/stencil/pallas_call | solution.py:431
  55.9 0.0 copy-done
  55.9 0.0 copy-start.1
  55.9 0.9 %copy-done.1 = f32[16,2,8,128]{3,2,1,0:T(8,128)S(1)} copy-done((f32[16,2,8,128]{3,2,1,0:T(8,128)S(1)}, f32[16,2,8,128]{3,2,1,0:T(8,128)}, u32[]{:S(2)}) %copy-start.1) | copy-done | bytes 131096
  56.8 5.2 %gradient.1 = (bf16[256,6400]{1,0:T(8,128)(2,1)}, f32[16,192,384]{2,1,0:T(8,128)}) custom-call(f32[32,8,128]{2,1,0:T(8,128)S(1)} %bitcast.68, s32[256,2]{1,0:T(8,128)S(1)} %copy.16.where, bf16[256,6400]{1,0:T(8,128)(2,1)S(1)} %copy-done, f32[16,192,384]{2,1,0:T(8,128)} %get-tuple-element.7.state), custom_call_target="tpu_custom_call" | custom-call | tf_op jit(solution)/shard_map/gradient/pallas_call | solution.py:547
  (7 shorter events, 0.1 us)
Async XLA Ops:
  3.5 52.4 %copy-start = (bf16[256,6400]{1,0:T(8,128)(2,1)S(1)}, bf16[256,6400]{1,0:T(8,128)(2,1)}, u32[]{:S(2)}) copy-start(bf16[256,6400]{1,0:T(8,128)(2,1)} %burn.1) | copy-start | bytes 9830404
  55.9 0.9 %copy-start.1 = (f32[16,2,8,128]{3,2,1,0:T(8,128)S(1)}, f32[16,2,8,128]{3,2,1,0:T(8,128)}, u32[]{:S(2)}) copy-start(f32[16,2,8,128]{3,2,1,0:T(8,128)} %get-tuple-element.6) | copy-start | bytes 393220
